TPU v7x, 32 devices: a whole 2x2x4 slice. The times are simulated.
32 devices in a mesh: dp: 4 (over y, x), tp: 8 (over z, core).
Axes of the slice: x: 2, y: 2, z: 4, core: 2. Of those that a mesh axis runs over, the one named last changes fastest.
Arguments:
- inputs: bfloat16 [16, 1024, 1024], P('dp', 'tp'), may hold values from -6 to 6
- memory: bfloat16 [16, 512, 1024], P('dp', 'tp'), may hold values from -6 to 6
- segments: int32 [16, 1024], P('dp', 'tp'), may hold values from 0 to 2, as said below
- memory_segments: int32 [16, 512], P('dp', 'tp'), may hold values from 0 to 2, as said below
- gain_self: float32 [1024], replicated, may hold values from 0.5 to 1.5
- gain_cross: float32 [1024], replicated, may hold values from 0.5 to 1.5
- gain_ffn: float32 [1024], replicated, may hold values from 0.5 to 1.5
- relative_bias: float32 [32, 16], replicated, may hold values from -4 to 4
- self_query: bfloat16 [1024, 1024], replicated, may hold values from -0.1875 to 0.1875
- self_key: bfloat16 [1024, 512], replicated, may hold values from -0.1875 to 0.1875
- self_value: bfloat16 [1024, 512], replicated, may hold values from -0.1875 to 0.1875
- self_out: bfloat16 [1024, 1024], replicated, may hold values from -1.5 to 1.5
- cross_query: bfloat16 [1024, 1024], replicated, may hold values from -0.1875 to 0.1875
- cross_key: bfloat16 [1024, 512], replicated, may hold values from -0.1875 to 0.1875
- cross_value: bfloat16 [1024, 512], replicated, may hold values from -0.1875 to 0.1875
- cross_out: bfloat16 [1024, 1024], replicated, may hold values from -1.5 to 1.5
- ffn_gate: bfloat16 [1024, 2816], P(None, 'tp'), may hold values from -0.1875 to 0.1875
- ffn_up: bfloat16 [1024, 2816], P(None, 'tp'), may hold values from -0.1875 to 0.1875
- ffn_down: bfloat16 [2816, 1024], P('tp'), may hold values from -0.15625 to 0.15625
- cotangent: bfloat16 [16, 1024, 1024], P('dp', 'tp'), may hold values from -6 to 6
Outputs:
- output: bfloat16 [16, 1024, 1024], P('dp', 'tp')
- input_grad: float32 [16, 1024, 1024], P('dp', 'tp')
- memory_grad: float32 [16, 512, 1024], P('dp', 'tp')
- gain_self_grad: float32 [1024], P(('dp', 'tp'))
- gain_cross_grad: float32 [1024], P(('dp', 'tp'))
- gain_ffn_grad: float32 [1024], P(('dp', 'tp'))
- relative_grad: float32 [512], P(('dp', 'tp'))
- self_query_grad: float32 [1024, 1024], P(('dp', 'tp'))
- self_key_grad: float32 [1024, 512], P(('dp', 'tp'))
- self_value_grad: float32 [1024, 512], P(('dp', 'tp'))
- self_out_grad: float32 [1024, 1024], P(('dp', 'tp'))
- cross_query_grad: float32 [1024, 1024], P(('dp', 'tp'))
- cross_key_grad: float32 [1024, 512], P(('dp', 'tp'))
- cross_value_grad: float32 [1024, 512], P(('dp', 'tp'))
- cross_out_grad: float32 [1024, 1024], P(('dp', 'tp'))
- ffn_gate_grad: float32 [1024, 2816], P('dp', 'tp')
- ffn_up_grad: float32 [1024, 2816], P('dp', 'tp')
- ffn_down_grad: float32 [2816, 1024], P('tp', 'dp')
Inputs may be any that keep to these rules, and one draw needn't show every extreme that they name: `segments`: along each row the ids never fall, and each of 0, 1 and 2 appears. `memory_segments`: along each row the ids never fall, and each of 0, 1 and 2 appears.
All inputs are finite; a program needn't handle non-finite values.
Results may differ from a plain program's by a relative error of at most 0.025.
Values may be sent and summed in bfloat16 or wider, within the bound.
A program may use at most 320 MiB of HBM per device.

v0:
```python
import math

import jax
import jax.numpy as jnp
from jax import lax
from jax.sharding import PartitionSpec as P

HEADS = 16
HEAD_DIM = 64
GROUPS = 8
BUCKETS = 32
MAX_DIST = 128


norm_epsilon = 1e-06
highest = lax.Precision.HIGHEST


def root_norm(operand, gain_vector):
    return (
        operand
        * lax.rsqrt(jnp.mean(operand * operand, axis=-1, keepdims=True) + norm_epsilon)
        * gain_vector
    )


def bucket_of(distance):
    exact = BUCKETS // 2
    bucket_count = jnp.zeros_like(distance)
    for step_index in range(1, exact):
        threshold = math.ceil(exact * (MAX_DIST / exact) ** (step_index / exact))
        bucket_count = bucket_count + (distance >= threshold).astype(jnp.int32)
    return jnp.where(distance < exact, distance, exact + bucket_count)


def gated(gate_pre, up_pre):
    return jax.nn.gelu(gate_pre, approximate=True) * up_pre


def project(left, right):
    return jnp.einsum("...i,io->...o", left, right, preferred_element_type=jnp.float32)


def project_back(left, right):
    return jnp.einsum("...o,io->...i", left, right, preferred_element_type=jnp.float32)


def weight_grad(inputs_held, grads_held):
    return jnp.einsum("rsi,rso->io", inputs_held, grads_held, preferred_element_type=jnp.float32)


def query_groups(queries):
    return queries.reshape(
        queries.shape[0], queries.shape[1], GROUPS, HEADS // GROUPS, HEAD_DIM
    ).transpose(2, 0, 3, 1, 4)


def query_merge(grouped):
    return grouped.transpose(1, 3, 0, 2, 4).reshape(
        grouped.shape[1], grouped.shape[3], HEADS * HEAD_DIM
    )


def key_groups(key_rows):
    return key_rows.reshape(key_rows.shape[0], key_rows.shape[1], GROUPS, HEAD_DIM).transpose(
        2, 0, 1, 3
    )


def key_merge(grouped):
    return grouped.transpose(1, 2, 0, 3).reshape(
        grouped.shape[1], grouped.shape[2], GROUPS * HEAD_DIM
    )


def group_scores(query_block, key_block, bias_block, allowed):
    scores = jnp.einsum(
        "rjqd,rkd->rjqk", query_block, key_block, preferred_element_type=jnp.float32
    )
    scores = scores * HEAD_DIM ** (-0.5) + bias_block
    return jnp.where(allowed[:, None], scores, -1e30)


def attend_forward(query_block, key_block, value_block, bias_block, allowed):
    scores = group_scores(query_block, key_block, bias_block, allowed)
    row_top = jnp.max(scores, axis=-1, keepdims=True)
    exponent = jnp.exp(scores - row_top)
    row_total = jnp.sum(exponent, axis=-1, keepdims=True)
    weights = (exponent / row_total).astype(jnp.bfloat16)
    context = jnp.einsum("rjqk,rkd->rjqd", weights, value_block, preferred_element_type=jnp.float32)
    return (context, row_top + jnp.log(row_total))


def attend_backward(query_block, key_block, value_block, bias_block, allowed, logsum, grad_context):
    scores = group_scores(query_block, key_block, bias_block, allowed)
    probabilities = jnp.exp(scores - logsum)
    grad_probs = jnp.einsum(
        "rjqd,rkd->rjqk", grad_context, value_block, preferred_element_type=jnp.float32
    )
    middle = jnp.sum(probabilities * grad_probs, axis=-1, keepdims=True)
    grad_scores = (probabilities * (grad_probs - middle)).astype(jnp.bfloat16)
    scale = HEAD_DIM ** (-0.5)
    grad_query = (
        jnp.einsum("rjqk,rkd->rjqd", grad_scores, key_block, preferred_element_type=jnp.float32)
        * scale
    )
    grad_key = (
        jnp.einsum("rjqk,rjqd->rkd", grad_scores, query_block, preferred_element_type=jnp.float32)
        * scale
    )
    grad_value = jnp.einsum(
        "rjqk,rjqd->rkd",
        probabilities.astype(jnp.bfloat16),
        grad_context,
        preferred_element_type=jnp.float32,
    )
    return (grad_query, grad_key, grad_value, grad_scores)


def on_device(
    inputs,
    memory,
    segments,
    memory_segments,
    gain_self,
    gain_cross,
    gain_ffn,
    relative_bias,
    self_query,
    self_key,
    self_value,
    self_out,
    cross_query,
    cross_key,
    cross_value,
    cross_out,
    ffn_gate,
    ffn_up,
    ffn_down,
    cotangent,
):
    seq_here = inputs.shape[1]
    tp_count = lax.axis_size("tp")
    row_len = seq_here * tp_count
    pair_width = GROUPS * HEAD_DIM
    stream = inputs.astype(jnp.float32)
    normed_self, self_norm_pull = jax.vjp(root_norm, stream, gain_self)
    held_self = normed_self.astype(jnp.bfloat16)
    queries = project(held_self, self_query).astype(jnp.bfloat16)
    key_rows = project(held_self, self_key).astype(jnp.bfloat16)
    value_rows = project(held_self, self_value).astype(jnp.bfloat16)
    memory_keys = project(memory, cross_key).astype(jnp.bfloat16)
    memory_values = project(memory, cross_value).astype(jnp.bfloat16)
    key_value = jnp.concatenate([key_rows, value_rows], axis=-1)
    memory_pairs = jnp.concatenate([memory_keys, memory_values], axis=-1)
    all_pairs, all_segments, all_memory_pairs, all_memory_segments = (
        lax.all_gather(key_value, "tp", axis=1, tiled=True),
        lax.all_gather(segments, "tp", axis=1, tiled=True),
        lax.all_gather(memory_pairs, "tp", axis=1, tiled=True),
        lax.all_gather(memory_segments, "tp", axis=1, tiled=True),
    )
    query_place = lax.axis_index("tp") * seq_here + jnp.arange(seq_here, dtype=jnp.int32)
    key_place = jnp.arange(row_len, dtype=jnp.int32)
    distance = jnp.maximum(query_place[:, None] - key_place[None, :], 0)
    onehot = (bucket_of(distance)[:, :, None] == jnp.arange(BUCKETS, dtype=jnp.int32)).astype(
        jnp.float32
    )
    bias_groups = jnp.einsum("qkb,bh->hqk", onehot, relative_bias, precision=highest)
    bias_groups = bias_groups.reshape(GROUPS, HEADS // GROUPS, seq_here, row_len)
    allowed_self = (segments[:, :, None] == all_segments[:, None, :]) & (
        query_place[:, None] >= key_place[None, :]
    )[None]
    self_groups = (
        query_groups(queries),
        key_groups(all_pairs[..., :pair_width]),
        key_groups(all_pairs[..., pair_width:]),
        bias_groups,
    )

    def self_forward(operands):
        return attend_forward(operands[0], operands[1], operands[2], operands[3], allowed_self)

    self_context_groups, self_logsum = lax.map(self_forward, self_groups)
    self_context = query_merge(self_context_groups).astype(jnp.bfloat16)
    stream_one = stream + project(self_context, self_out)
    normed_cross, cross_norm_pull = jax.vjp(root_norm, stream_one, gain_cross)
    held_cross = normed_cross.astype(jnp.bfloat16)
    cross_queries = project(held_cross, cross_query).astype(jnp.bfloat16)
    allowed_cross = segments[:, :, None] == all_memory_segments[:, None, :]
    cross_groups = (
        query_groups(cross_queries),
        key_groups(all_memory_pairs[..., :pair_width]),
        key_groups(all_memory_pairs[..., pair_width:]),
    )

    def cross_forward(operands):
        return attend_forward(operands[0], operands[1], operands[2], 0.0, allowed_cross)

    cross_context_groups, cross_logsum = lax.map(cross_forward, cross_groups)
    cross_context = query_merge(cross_context_groups).astype(jnp.bfloat16)
    stream_two = stream_one + project(cross_context, cross_out)
    normed_ffn, ffn_norm_pull = jax.vjp(root_norm, stream_two, gain_ffn)
    held_ffn = normed_ffn.astype(jnp.bfloat16)
    gate_full, up_full, down_full = (
        lax.all_gather(ffn_gate, "tp", axis=1, tiled=True),
        lax.all_gather(ffn_up, "tp", axis=1, tiled=True),
        lax.all_gather(ffn_down, "tp", axis=0, tiled=True),
    )
    hidden, gated_pull = jax.vjp(gated, project(held_ffn, gate_full), project(held_ffn, up_full))
    hidden = hidden.astype(jnp.bfloat16)
    stream_three = stream_two + project(hidden, down_full)
    grad_gate, grad_up = gated_pull(project_back(cotangent, down_full))
    grad_gate = grad_gate.astype(jnp.bfloat16)
    grad_up = grad_up.astype(jnp.bfloat16)
    gate_part, up_part, down_part = (
        lax.psum_scatter(
            weight_grad(held_ffn, grad_gate).astype(jnp.bfloat16),
            "tp",
            scatter_dimension=1,
            tiled=True,
        ).astype(jnp.float32),
        lax.psum_scatter(
            weight_grad(held_ffn, grad_up).astype(jnp.bfloat16),
            "tp",
            scatter_dimension=1,
            tiled=True,
        ).astype(jnp.float32),
        lax.psum_scatter(
            weight_grad(hidden, cotangent).astype(jnp.bfloat16),
            "tp",
            scatter_dimension=0,
            tiled=True,
        ).astype(jnp.float32),
    )
    grad_held_ffn = project_back(grad_gate, gate_full) + project_back(grad_up, up_full)
    output = stream_three.astype(jnp.bfloat16)
    ffn_gate_grad, ffn_up_grad, ffn_down_grad = (
        lax.psum_scatter(
            gate_part.astype(jnp.bfloat16), "dp", scatter_dimension=0, tiled=True
        ).astype(jnp.float32),
        lax.psum_scatter(
            up_part.astype(jnp.bfloat16), "dp", scatter_dimension=0, tiled=True
        ).astype(jnp.float32),
        lax.psum_scatter(
            down_part.astype(jnp.bfloat16), "dp", scatter_dimension=1, tiled=True
        ).astype(jnp.float32),
    )
    grad_stream_part, gain_ffn_part = ffn_norm_pull(grad_held_ffn)
    grad_two = cotangent.astype(jnp.float32) + grad_stream_part
    cross_branch = grad_two.astype(jnp.bfloat16)
    cross_out_part = weight_grad(cross_context, cross_branch)
    grad_cross_context = project_back(cross_branch, cross_out).astype(jnp.bfloat16)

    def cross_backward(operands):
        grad_query, grad_key, grad_value, grad_scores = attend_backward(
            operands[0], operands[1], operands[2], 0.0, allowed_cross, operands[3], operands[4]
        )
        return (grad_query, grad_key, grad_value)

    cross_query_groups, memory_key_groups, memory_value_groups = lax.map(
        cross_backward, cross_groups + (cross_logsum, query_groups(grad_cross_context))
    )
    grad_cross_queries = query_merge(cross_query_groups).astype(jnp.bfloat16)
    grad_memory_pairs = jnp.concatenate(
        [key_merge(memory_key_groups), key_merge(memory_value_groups)], axis=-1
    )
    cross_query_part = weight_grad(held_cross, grad_cross_queries)
    grad_stream_part, gain_cross_part = cross_norm_pull(
        project_back(grad_cross_queries, cross_query)
    )
    grad_one = grad_two + grad_stream_part
    self_branch = grad_one.astype(jnp.bfloat16)
    self_out_part = weight_grad(self_context, self_branch)
    grad_self_context = project_back(self_branch, self_out).astype(jnp.bfloat16)

    def self_backward(operands):
        grad_query, grad_key, grad_value, grad_scores = attend_backward(
            operands[0],
            operands[1],
            operands[2],
            operands[3],
            allowed_self,
            operands[4],
            operands[5],
        )
        return (grad_query, grad_key, grad_value, jnp.sum(grad_scores.astype(jnp.float32), axis=0))

    query_grad_groups, key_grad_groups, value_grad_groups, bias_grad_groups = lax.map(
        self_backward, self_groups + (self_logsum, query_groups(grad_self_context))
    )
    grad_queries = query_merge(query_grad_groups).astype(jnp.bfloat16)
    bias_grad = bias_grad_groups.reshape(HEADS, seq_here, row_len)
    relative_part = jnp.einsum("qkb,hqk->bh", onehot, bias_grad, precision=highest).reshape(-1)
    grad_pairs = jnp.concatenate(
        [key_merge(key_grad_groups), key_merge(value_grad_groups)], axis=-1
    )
    pair_share, memory_share = (
        lax.psum_scatter(
            grad_pairs.astype(jnp.bfloat16), "tp", scatter_dimension=1, tiled=True
        ).astype(jnp.float32),
        lax.psum_scatter(
            grad_memory_pairs.astype(jnp.bfloat16), "tp", scatter_dimension=1, tiled=True
        ).astype(jnp.float32),
    )
    pair_held = pair_share.astype(jnp.bfloat16)
    memory_held = memory_share.astype(jnp.bfloat16)
    self_query_part = weight_grad(held_self, grad_queries)
    self_key_part = weight_grad(held_self, pair_held[..., :pair_width])
    self_value_part = weight_grad(held_self, pair_held[..., pair_width:])
    grad_held_self = (
        project_back(grad_queries, self_query)
        + project_back(pair_held[..., :pair_width], self_key)
        + project_back(pair_held[..., pair_width:], self_value)
    )
    grad_stream_part, gain_self_part = self_norm_pull(grad_held_self)
    input_grad = grad_one + grad_stream_part
    cross_key_part = weight_grad(memory, memory_held[..., :pair_width])
    cross_value_part = weight_grad(memory, memory_held[..., pair_width:])
    memory_grad = project_back(memory_held[..., :pair_width], cross_key) + project_back(
        memory_held[..., pair_width:], cross_value
    )
    (
        gain_self_grad,
        gain_cross_grad,
        gain_ffn_grad,
        relative_grad,
        self_query_grad,
        self_key_grad,
        self_value_grad,
        self_out_grad,
        cross_query_grad,
        cross_key_grad,
        cross_value_grad,
        cross_out_grad,
    ) = (
        lax.psum_scatter(gain_self_part, ("dp", "tp"), scatter_dimension=0, tiled=True),
        lax.psum_scatter(gain_cross_part, ("dp", "tp"), scatter_dimension=0, tiled=True),
        lax.psum_scatter(gain_ffn_part, ("dp", "tp"), scatter_dimension=0, tiled=True),
        lax.psum_scatter(relative_part, ("dp", "tp"), scatter_dimension=0, tiled=True),
        lax.psum_scatter(self_query_part, ("dp", "tp"), scatter_dimension=0, tiled=True),
        lax.psum_scatter(self_key_part, ("dp", "tp"), scatter_dimension=0, tiled=True),
        lax.psum_scatter(self_value_part, ("dp", "tp"), scatter_dimension=0, tiled=True),
        lax.psum_scatter(self_out_part, ("dp", "tp"), scatter_dimension=0, tiled=True),
        lax.psum_scatter(cross_query_part, ("dp", "tp"), scatter_dimension=0, tiled=True),
        lax.psum_scatter(cross_key_part, ("dp", "tp"), scatter_dimension=0, tiled=True),
        lax.psum_scatter(cross_value_part, ("dp", "tp"), scatter_dimension=0, tiled=True),
        lax.psum_scatter(cross_out_part, ("dp", "tp"), scatter_dimension=0, tiled=True),
    )
    return (
        output,
        input_grad,
        memory_grad,
        gain_self_grad,
        gain_cross_grad,
        gain_ffn_grad,
        relative_grad,
        self_query_grad,
        self_key_grad,
        self_value_grad,
        self_out_grad,
        cross_query_grad,
        cross_key_grad,
        cross_value_grad,
        cross_out_grad,
        ffn_gate_grad,
        ffn_up_grad,
        ffn_down_grad,
    )


def solution(mesh):
    placed = (
        P("dp", "tp", None),
        P("dp", "tp", None),
        P("dp", "tp"),
        P("dp", "tp"),
        P(),
        P(),
        P(),
        P(),
        P(),
        P(),
        P(),
        P(),
        P(),
        P(),
        P(),
        P(),
        P(None, "tp"),
        P(None, "tp"),
        P("tp", None),
        P("dp", "tp", None),
    )
    return jax.shard_map(
        on_device,
        mesh=mesh,
        in_specs=placed,
        out_specs=(
            P("dp", "tp", None),
            P("dp", "tp", None),
            P("dp", "tp", None),
            P(("dp", "tp")),
            P(("dp", "tp")),
            P(("dp", "tp")),
            P(("dp", "tp")),
            P(("dp", "tp"), None),
            P(("dp", "tp"), None),
            P(("dp", "tp"), None),
            P(("dp", "tp"), None),
            P(("dp", "tp"), None),
            P(("dp", "tp"), None),
            P(("dp", "tp"), None),
            P(("dp", "tp"), None),
            P("dp", "tp"),
            P("dp", "tp"),
            P("tp", "dp"),
        ),
        check_vma=False,
    )
```

profile of v0, /device:TPU:0, one launch (start us, length us, event | category | flops | bytes accessed | tf_op | source)
XLA Modules:
  0.0 1955.3 jit_solution(13104001282129523883)
XLA Ops:
  34.1 74.9 %copy.181 = pred[128,1024,32]{1,2,0:T(32,128)(4,1)S(1)} copy(pred[128,1024,32]{0,2,1:T(32,128)(4,1)S(1)} %iota_compare_fusion) | data formatting | bytes 8388608 | tf_op jit(solution)/shard_map/eq | solution.py:165
  115.3 8.1 copy.265
  123.4 14.5 all_gather.21
  137.9 12.8 all-gather
  170.0 8.8 fusion.109
  178.9 26.5 %all-gather.7.cloned.1.call-done = bf16[4,1024,1024]{2,1,0:T(8,128)(2,1)} async-done(((bf16[4,128,1024]{2,1,0:T(8,128)(2,1)}), bf16[4,1024,1024]{2,1,0:T(8,128)(2,1)}) %all-gather.7.cloned.1.call-update) | async-done | bytes 8388624 | tf_op jit(solution)/shard_map/all_gather | solution.py:157
  211.2 6.6 copy.179
  222.7 6.3 copy.182
  235.2 71.6 %while.58 = (s32[]{:T(128)}, bf16[8,4,2,128,64]{3,4,2,0,1:T(8,128)(2,1)}, f32[8,4,2,128,1]{3,2,1,4,0:T(2,128)S(1)}, bf16[8,4,2,128,64]{3,4,2,1,0:T(8,128)(2,1)},...) while((s32[]{:T(128)}, ...), condition=%wide.region_4.5_spmd.clone, body=%wide.region_1.4_spmd.clone.sunk | while | flops 285211648 | bytes 21549180 | solution.py:183
  317.1 39.8 %while.59 = (s32[]{:T(128)}, bf16[8,4,2,128,64]{3,4,2,0,1:T(8,128)(2,1)}, f32[8,4,2,128,1]{3,2,1,4,0:T(2,128)S(1)}, bf16[8,4,2,128,64]{3,4,2,1,0:T(8,128)(2,1)S(...) while((s32[]{:T(128)}, ...), condition=%wide.region_9.10_spmd.clone, body=%wide.region_6.9_spmd.clone.sunk | while | flops 140770304 | bytes 8302697 | solution.py:199
  363.4 8.6 fusion.115
  372.0 14.2 fusion.108
  393.1 7.8 bitcast_convert_fusion.1
  420.0 7.8 bitcast_convert_fusion
  429.1 71.5 %while.60 = (s32[]{:T(128)}, bf16[8,4,2,128,64]{3,4,2,0,1:T(8,128)(2,1)}, bf16[8,4,512,64]{2,3,0,1:T(8,128)(2,1)}, bf16[8,4,512,64]{2,3,0,1:T(8,128)(2,1)}, bf16...) while((s32[]{:T(128)}, ...), condition=%wide.region_14.15_spmd.clone, body=%wide.region_12.14_spmd.clone.sunk | while | flops 340720640 | bytes 18910336 | solution.py:260
  525.0 114.2 %while.61 = (s32[]{:T(128)}, bf16[8,4,2,128,64]{3,4,2,0,1:T(8,128)(2,1)}, bf16[8,4,1024,64]{2,3,0,1:T(8,128)(2,1)}, bf16[8,4,1024,64]{2,3,0,1:T(8,128)(2,1)}, f3...) while((s32[]{:T(128)}, ...), condition=%wide.region_19.20_spmd.clone, body=%wide.region_16.19_spmd.clone.sunk | while | flops 684784640 | bytes 43429024 | solution.py:288
  651.6 7.8 pad_maximum_fusion
  694.3 53.3 %reduce-scatter.21.cloned.1.call-done = bf16[4,128,1024]{2,1,0:T(8,128)(2,1)} async-done(((bf16[4,1024,1024]{2,1,0:T(8,128)(2,1)}), bf16[4,128,1024]{2,1,0:T(8,128)(2,1)}) %reduce-scatter.21.cloned.1.call-update) | async-done | bytes 1048592 | tf_op jit(solution)/shard_map/reduce_scatter | solution.py:298
  754.2 9.3 copy.221
  763.6 11.1 convolution_bitcast_fusion.13
  779.5 6.9 add_convert_fusion
  790.7 12.8 reduce-scatter.43.cloned.1.call-done
  805.2 27.0 %reduce-scatter.47.cloned.1.call-done = bf16[352,256]{1,0:T(8,128)(2,1)} async-done(((bf16[352,1024]{1,0:T(8,128)(2,1)}), bf16[352,256]{1,0:T(8,128)(2,1)}) %reduce-scatter.47.cloned.1.call-update) | async-done | bytes 180240 | tf_op jit(solution)/shard_map/reduce_scatter | solution.py:244
  838.6 40.3 %all-reduce.4 = (f32[1024]{0:T(1024)S(1)}, f32[1024]{0:T(1024)S(1)}, f32[1024]{0:T(1024)S(1)}, f32[512]{0:T(512)S(1)}) all-reduce(f32[1024]{0:T(1024)S(1)} %get-tuple-element.562, f32[1024]{0:T(1024)S(1)} %get-tuple-element.560, f32[1024]{0:T(1024)S(1)} %copy-done.32, ...), channel_id=4, replica_groups=mesh['dp'=4,'tp'=8] {'dp','tp'}, use_global_device_ids=true, to_apply=%region_24.25.clone | all-reduce | flops 3584 | bytes 28672
  885.4 91.6 %reduce-scatter.25.cloned.1.call-done = f32[32,1024]{1,0:T(8,128)} async-done(((f32[1024,1024]{1,0:T(8,128)}), f32[32,1024]{1,0:T(8,128)}) %reduce-scatter.25.cloned.1.call-update) | async-done | bytes 131088 | tf_op jit(solution)/shard_map/reduce_scatter | solution.py:340
  977.0 142.9 %reduce-scatter.31.cloned.1.call-done = f32[32,1024]{1,0:T(8,128)} async-done(((f32[1024,1024]{1,0:T(8,128)}), f32[32,1024]{1,0:T(8,128)}) %reduce-scatter.31.cloned.1.call-update) | async-done | bytes 131088 | tf_op jit(solution)/shard_map/reduce_scatter | solution.py:343
  1120.0 141.8 %reduce-scatter.33.cloned.1.call-done = f32[32,1024]{1,0:T(8,128)} async-done(((f32[1024,1024]{1,0:T(8,128)}), f32[32,1024]{1,0:T(8,128)}) %reduce-scatter.33.cloned.1.call-update) | async-done | bytes 131088 | tf_op jit(solution)/shard_map/reduce_scatter | solution.py:344
  1261.8 142.4 %reduce-scatter.35.cloned.1.call-done = f32[32,1024]{1,0:T(8,128)} async-done(((f32[1024,1024]{1,0:T(8,128)}), f32[32,1024]{1,0:T(8,128)}) %reduce-scatter.35.cloned.1.call-update) | async-done | bytes 131088 | tf_op jit(solution)/shard_map/reduce_scatter | solution.py:347
  1404.2 136.2 %reduce-scatter.49.cloned.1.call-done = f32[32,512]{1,0:T(8,128)} async-done(((f32[1024,512]{1,0:T(8,128)}), f32[32,512]{1,0:T(8,128)}) %reduce-scatter.49.cloned.1.call-update) | async-done | bytes 65552
  1540.4 136.1 %reduce-scatter.51.cloned.1.call-done = f32[32,512]{1,0:T(8,128)} async-done(((f32[1024,512]{1,0:T(8,128)}), f32[32,512]{1,0:T(8,128)}) %reduce-scatter.51.cloned.1.call-update) | async-done | bytes 65552
  1676.5 135.3 %reduce-scatter.27.cloned.1.call-done = f32[32,512]{1,0:T(8,128)} async-done(((f32[1024,512]{1,0:T(8,128)}), f32[32,512]{1,0:T(8,128)}) %reduce-scatter.27.cloned.1.call-update) | async-done | bytes 65552 | tf_op jit(solution)/shard_map/reduce_scatter | solution.py:341
  1811.8 136.4 %reduce-scatter.29.cloned.1.call-done = f32[32,512]{1,0:T(8,128)} async-done(((f32[1024,512]{1,0:T(8,128)}), f32[32,512]{1,0:T(8,128)}) %reduce-scatter.29.cloned.1.call-update) | async-done | bytes 65552 | tf_op jit(solution)/shard_map/reduce_scatter | solution.py:342
  (445 shorter events, 510.8 us)
Async XLA Ops:
  7.2 304.3 %copy-start = (bf16[1024,1024]{1,0:T(8,128)(2,1)S(1)}, bf16[1024,1024]{1,0:T(8,128)(2,1)}, u32[]{:S(2)}) copy-start(bf16[1024,1024]{1,0:T(8,128)(2,1)} %param.40) | copy-start | bytes 6291460
  7.2 143.6 %all-gather.9.cloned.1.call-start = ((), (), s32[]{:S(2)}) async-start(), calls=%async_computation.17 | async-start | bytes 4718592 | tf_op jit(solution)/shard_map/all_gather | solution.py:159
  12.0 158.0 %all-gather.15.cloned.1.call-start = ((), (), s32[]{:S(2)}) async-start(), calls=%async_computation.20 | async-start | bytes 6488064 | tf_op jit(solution)/shard_map/all_gather | solution.py:207
  12.8 192.6 %all-gather.7.cloned.1.call-start = ((), (), s32[]{:S(2)}) async-start(), calls=%async_computation.16 | async-start | bytes 9437184 | tf_op jit(solution)/shard_map/all_gather | solution.py:157
  13.2 7.1 copy-start.23
  17.2 346.2 %all-gather.13.cloned.1.call-start = ((), (), s32[]{:S(2)}) async-start(), calls=%async_computation.19 | async-start | bytes 6488064 | tf_op jit(solution)/shard_map/all_gather | solution.py:206
  17.8 354.2 %all-gather.11.cloned.1.call-start = ((), (), s32[]{:S(2)}) async-start(), calls=%async_computation.18 | async-start | bytes 6488064 | tf_op jit(solution)/shard_map/all_gather | solution.py:205
  18.3 641.2 %reduce-scatter.37.cloned.1.call-start = ((), (), s32[]{:S(2)}) async-start(), calls=%async_computation.29 | async-start | bytes 6488064 | tf_op jit(solution)/shard_map/reduce_scatter | solution.py:216
  34.1 74.9 %copy-start.30 = (f32[32,16]{0,1:T(8,128)S(1)}, f32[32,16]{0,1:T(8,128)}, u32[]{:S(2)}) copy-start(f32[32,16]{0,1:T(8,128)} %param.35) | copy-start | bytes 6148
  115.2 8.1 copy-start.21
  115.2 22.6 %copy-start.33 = (s32[4,64]{1,0:T(4,128)S(1)}, s32[4,64]{1,0:T(4,128)}, u32[]{:S(2)}) copy-start(s32[4,64]{1,0:T(4,128)} %param.31) | copy-start | bytes 3076
  372.0 15.8 copy-start.19
  392.8 267.5 %reduce-scatter.41.cloned.1.call-start = ((), (), s32[]{:S(2)}) async-start(), calls=%async_computation.31 | async-start | bytes 6488064 | tf_op jit(solution)/shard_map/reduce_scatter | solution.py:222
  400.9 260.0 %reduce-scatter.45.cloned.1.call-start = ((), (), s32[]{:S(2)}) async-start(), calls=%async_computation.33 | async-start | bytes 6488064 | tf_op jit(solution)/shard_map/reduce_scatter | solution.py:228
  401.0 6.2 copy-start.4
  407.2 6.3 copy-start.20
  427.8 254.6 %reduce-scatter.23.cloned.1.call-start = ((), (), s32[]{:S(2)}) async-start(), calls=%async_computation.22 | async-start | bytes 4718592 | tf_op jit(solution)/shard_map/reduce_scatter | solution.py:301
  523.3 224.4 %reduce-scatter.21.cloned.1.call-start = ((), (), s32[]{:S(2)}) async-start(), calls=%async_computation.21 | async-start | bytes 9437184 | tf_op jit(solution)/shard_map/reduce_scatter | solution.py:298
  659.5 129.5 %reduce-scatter.39.cloned.1.call-start = ((), (), s32[]{:S(2)}) async-start(), calls=%async_computation.30 | async-start | bytes 901120 | tf_op jit(solution)/shard_map/reduce_scatter | solution.py:238
  660.2 143.2 %reduce-scatter.43.cloned.1.call-start = ((), (), s32[]{:S(2)}) async-start(), calls=%async_computation.32 | async-start | bytes 901120 | tf_op jit(solution)/shard_map/reduce_scatter | solution.py:241
  660.8 171.3 %reduce-scatter.47.cloned.1.call-start = ((), (), s32[]{:S(2)}) async-start(), calls=%async_computation.34 | async-start | bytes 901120 | tf_op jit(solution)/shard_map/reduce_scatter | solution.py:244
  661.6 315.4 %reduce-scatter.25.cloned.1.call-start = ((), (), s32[]{:S(2)}) async-start(), calls=%async_computation.23 | async-start | bytes 4325376 | tf_op jit(solution)/shard_map/reduce_scatter | solution.py:340
  666.4 453.6 %reduce-scatter.31.cloned.1.call-start = ((), (), s32[]{:S(2)}) async-start(), calls=%async_computation.26 | async-start | bytes 4325376 | tf_op jit(solution)/shard_map/reduce_scatter | solution.py:343
  671.7 590.1 %reduce-scatter.33.cloned.1.call-start = ((), (), s32[]{:S(2)}) async-start(), calls=%async_computation.27 | async-start | bytes 4325376 | tf_op jit(solution)/shard_map/reduce_scatter | solution.py:344
  677.1 727.1 %reduce-scatter.35.cloned.1.call-start = ((), (), s32[]{:S(2)}) async-start(), calls=%async_computation.28 | async-start | bytes 4325376 | tf_op jit(solution)/shard_map/reduce_scatter | solution.py:347
  682.3 858.1 %reduce-scatter.49.cloned.1.call-start = ((), (), s32[]{:S(2)}) async-start(), calls=%async_computation.35 | async-start | bytes 2162688
  688.2 988.3 %reduce-scatter.51.cloned.1.call-start = ((), (), s32[]{:S(2)}) async-start(), calls=%async_computation.36 | async-start | bytes 2162688
  694.3 1117.5 %reduce-scatter.27.cloned.1.call-start = ((), (), s32[]{:S(2)}) async-start(), calls=%async_computation.24 | async-start | bytes 2162688 | tf_op jit(solution)/shard_map/reduce_scatter | solution.py:341
  750.9 1197.3 %reduce-scatter.29.cloned.1.call-start = ((), (), s32[]{:S(2)}) async-start(), calls=%async_computation.25 | async-start | bytes 2162688 | tf_op jit(solution)/shard_map/reduce_scatter | solution.py:342
  779.5 6.9 copy-start.11
  779.5 6.9 copy-start.22
  836.1 45.2 %copy-start.26 = (f32[4,128]{1,0:T(4,128)S(1)}, f32[4,128]{1,0:T(4,128)}, u32[]{:S(2)}) copy-start(f32[4,128]{1,0:T(4,128)} %copy-done.25) | copy-start | bytes 6148
  (26 other events, 76.4 us)
Sparse Core Ops, SparseCore 0:
  12.2 49.8 all-gather.8
  63.7 59.0 all-gather.14
  124.4 80.8 all-gather.6
  206.9 58.9 all-gather.12
  267.4 59.0 all-gather.10
  393.0 63.2 reduce-scatter.36
  458.6 63.2 reduce-scatter.40
  524.1 63.2 reduce-scatter.44
  589.7 48.3 reduce-scatter.22
  659.6 88.0 reduce-scatter.20
  750.6 24.0 reduce-scatter.38
  777.7 25.7 reduce-scatter.42
  806.3 25.7 reduce-scatter.46
  834.9 142.0 reduce-scatter.24
  979.8 140.1 reduce-scatter.30
  1122.8 138.9 reduce-scatter.32
  1264.6 139.5 reduce-scatter.34
  1407.0 133.3 reduce-scatter.48
  1543.2 133.2 reduce-scatter.50
  1679.3 132.5 reduce-scatter.26
  1814.7 133.5 reduce-scatter.28
where the time goes:
time: 1970 us; the launch traced here: 1960 us
  waiting for transfers between devices  1190 us (60%)
  matrix products  393 us (20%)
  local copies, waits for them, and re-layouts  226 us (11%)
  blocking collectives  67.7 us (3%)
  other arithmetic  64.6 us (3%)
    unnamed x23, waiting for transfers between devices  276 us
    reduce_scatter x1, waiting for transfers between devices, on_device(): lax.psum_scatter(self_out_part, ('dp', 'tp'), scatter_dimension=0, tiled=...  143 us
    reduce_scatter x1, waiting for transfers between devices, on_device(): lax.psum_scatter(cross_out_part, ('dp', 'tp'), scatter_dimension=0, tiled...  142 us
    reduce_scatter x1, waiting for transfers between devices, on_device(): lax.psum_scatter(cross_query_part, ('dp', 'tp'), scatter_dimension=0, til...  142 us
    reduce_scatter x1, waiting for transfers between devices, on_device(): lax.psum_scatter(self_value_part, ('dp', 'tp'), scatter_dimension=0, tile...  136 us
    reduce_scatter x1, waiting for transfers between devices, on_device(): lax.psum_scatter(self_key_part, ('dp', 'tp'), scatter_dimension=0, tiled=...  135 us
    reduce_scatter x1, waiting for transfers between devices, on_device(): lax.psum_scatter(self_query_part, ('dp', 'tp'), scatter_dimension=0, tile...  91.6 us
    eq x1, local copies, waits for them, and re-layouts, on_device(): bucket_of(distance)[:, :, None] == jnp.arange(BUCKETS, dtype=jnp.int32)  74.9 us
  transfers between devices with their start and end apart: 21, of which 12 were waited for; matrix products, arithmetic and copies ran while one was open for 33% of the time, Pallas kernels for 0%

commit v1 on v0

v1 whole, which is shorter than its diff:
```python
import functools
import math

import jax
import jax.numpy as jnp
from jax import lax
from jax.experimental import pallas as pl
from jax.experimental.pallas import tpu as pltpu
from jax.sharding import PartitionSpec as P

HEADS = 16
HEAD_DIM = 64
GROUPS = 8
BUCKETS = 32
MAX_DIST = 128
BLOCK = 128
PAIRS = GROUPS // 2
FAR = -1e30
SCALE = HEAD_DIM ** (-0.5)
MIB = 1 << 20

norm_epsilon = 1e-06
f32 = jnp.float32
bf16 = jnp.bfloat16


def nn(left, right):
    return lax.dot_general(left, right, (((1,), (0,)), ((), ())), preferred_element_type=f32)


def nt(left, right):
    return lax.dot_general(left, right, (((1,), (1,)), ((), ())), preferred_element_type=f32)


def tn(left, right):
    return lax.dot_general(left, right, (((0,), (0,)), ((), ())), preferred_element_type=f32)


def bits_of(count):
    return count.bit_length() - 1


def xor_static(value, flips, count):
    result = value
    for bit in range(bits_of(count)):
        if flips >> bit & 1:
            result = result + (1 << bit) * (1 - 2 * ((value // (1 << bit)) % 2))
    return result


def half_order(count, first_low):
    nb = bits_of(count)
    bits = list(range(nb)) if first_low else list(range(nb))[::-1]
    order = []
    for index in range(count):
        s = 0
        for place, bit in enumerate(bits):
            if index >> (nb - 1 - place) & 1:
                s |= 1 << bit
        order.append(s)
    return order, bits


def norm_scale(v):
    return lax.rsqrt(jnp.mean(v * v, axis=-1, keepdims=True) + norm_epsilon)


def norm_back(v, gain, dy):
    s = norm_scale(v)
    gained = dy * gain
    grad = s * gained - v * (s * s * s * jnp.mean(gained * v, axis=-1, keepdims=True))
    return grad, jnp.sum(dy * v * s, axis=0)


def bucket_of(distance):
    exact = BUCKETS // 2
    bucket_count = jnp.zeros_like(distance)
    for step_index in range(1, exact):
        threshold = math.ceil(exact * (MAX_DIST / exact) ** (step_index / exact))
        bucket_count = bucket_count + (distance >= threshold).astype(jnp.int32)
    return jnp.where(distance < exact, distance, exact + bucket_count)


def whole_vmem():
    return pl.BlockSpec(memory_space=pltpu.VMEM)


def whole_smem():
    return pl.BlockSpec(memory_space=pltpu.SMEM)


def any_space():
    return pl.BlockSpec(memory_space=pl.ANY)


def params(limit_mib, **more):
    return pltpu.CompilerParams(vmem_limit_bytes=limit_mib * MIB, **more)


class Places:
    def __init__(self, rows):
        self.tp = lax.axis_size("tp")
        self.dp = lax.axis_size("dp")
        self.rows = rows
        self.share = self.tp // rows
        self.z_count = self.tp // 2

    def row(self):
        return lax.axis_index("tp") // self.share

    def part(self):
        return lax.axis_index("tp") % self.share

    def row_perm(self, k):
        share = self.share
        return [(t, ((t // share) ^ k) * share + t % share) for t in range(self.tp)]

    def part_perm(self, shift):
        share = self.share
        return [
            (t // share * share + (t % share + shift) % share, t) for t in range(self.tp)
        ]

    def core_perm(self):
        return [(t, t ^ 1) for t in range(self.tp)]

    def z_perm(self, shift):
        z_count = self.z_count
        return [(t, (t // 2 + shift) % z_count * 2 + t % 2) for t in range(self.tp)]

    def dp_perm(self, flips):
        return [(d, d ^ flips) for d in range(self.dp)]


def exchange_rows(at, array):
    row = at.row()
    received = []
    for k in range(1, at.rows):
        chunk = lax.dynamic_index_in_dim(array, xor_static(row, k, at.rows), 0, keepdims=False)
        received.append(lax.ppermute(chunk, "tp", at.row_perm(k)))
    return received


def place_kernel(at, *refs):
    own, pieces, out, sems = refs[0], refs[1 : at.rows], refs[at.rows], refs[at.rows + 1]
    row = at.row()
    copies = [pltpu.make_async_copy(own.at[row], out.at[row], sems.at[0])]
    for k in range(1, at.rows):
        copies.append(
            pltpu.make_async_copy(
                pieces[k - 1], out.at[xor_static(row, k, at.rows)], sems.at[k]
            )
        )
    for copy in copies:
        copy.start()
    for copy in copies:
        copy.wait()


def place_rows(at, own, pieces):
    return pl.pallas_call(
        functools.partial(place_kernel, at),
        out_shape=jax.ShapeDtypeStruct(own.shape, own.dtype),
        in_specs=[any_space()] * at.rows,
        out_specs=any_space(),
        scratch_shapes=[pltpu.SemaphoreType.DMA((at.rows,))],
        name="place_rows",
    )(own, *pieces)


def place_wide_kernel(at, *refs):
    own, pieces, out = refs[0], refs[1 : at.rows], refs[at.rows]
    row = at.row()
    out[row] = own[row].astype(f32)
    for k in range(1, at.rows):
        out[xor_static(row, k, at.rows)] = pieces[k - 1][...].astype(f32)


def place_wide(at, own, pieces):
    return pl.pallas_call(
        functools.partial(place_wide_kernel, at),
        out_shape=jax.ShapeDtypeStruct(own.shape, f32),
        in_specs=[whole_vmem()] * at.rows,
        out_specs=whole_vmem(),
        compiler_params=params(24),
        name="place_wide",
    )(own, *pieces)


def exchange_segments(at, packed):
    row = at.row()
    pieces = [lax.dynamic_index_in_dim(packed, row, 0, keepdims=False)]
    pieces += exchange_rows(at, packed)
    blocks = jnp.stack(pieces)
    for bit in range(bits_of(at.rows)):
        grouped = blocks.reshape(-1, 2, 1 << bit, blocks.shape[-1])
        flipped = grouped[:, ::-1]
        blocks = jnp.where((row // (1 << bit)) % 2 == 1, flipped, grouped).reshape(blocks.shape)
    return [blocks] + [
        lax.ppermute(blocks, "tp", at.part_perm(s)) for s in range(1, at.share)
    ]


def near_kinds(share):
    kinds = [(s, 0) for s in range(share)]
    return kinds + [(s, 1) for s in range(share) if s > 0 or share == 1]


def kind_distance(at, kind):
    s, back = kind
    part = at.part()
    return part - (part + s) % at.share + at.share * back


def tile_distance(at, kind):
    key = lax.broadcasted_iota(jnp.int32, (BLOCK, BLOCK), 0)
    query = lax.broadcasted_iota(jnp.int32, (BLOCK, BLOCK), 1)
    return BLOCK * kind_distance(at, kind) + query - key


def bias_tiles_kernel(at, table, out):
    group = pl.program_id(0)
    for number, kind in enumerate(near_kinds(at.share)):
        distance = tile_distance(at, kind)
        bucket = bucket_of(jnp.maximum(distance, 0))
        for j in range(2):
            head = group * 2 + j
            last = table[(BUCKETS - 1) * HEADS + head]
            value = jnp.zeros((BLOCK, BLOCK), f32)
            for b in range(BUCKETS - 1):
                value = jnp.where(bucket == b, table[b * HEADS + head] - last, value)
            out[0, number, :, j * BLOCK : (j + 1) * BLOCK] = jnp.where(distance < 0, FAR, value)


def bias_tiles(at, table):
    kinds = len(near_kinds(at.share))
    return pl.pallas_call(
        functools.partial(bias_tiles_kernel, at),
        grid=(GROUPS,),
        out_shape=jax.ShapeDtypeStruct((GROUPS, kinds, BLOCK, 2 * BLOCK), f32),
        in_specs=[whole_smem()],
        out_specs=pl.BlockSpec((1, kinds, BLOCK, 2 * BLOCK), lambda g: (g, 0, 0, 0)),
        name="bias_tiles",
    )(table)


def query_features(seg_block, last_parts, group):
    shape = (HEAD_DIM, 2 * BLOCK)
    row = lax.broadcasted_iota(jnp.int32, shape, 0)
    seg = jnp.concatenate([seg_block, seg_block], axis=1)
    feature = jnp.where((row < 3) & (seg != row), FAR, 0.0)
    if last_parts is not None:
        lane = lax.broadcasted_iota(jnp.int32, shape, 1)
        for part in range(3):
            first = last_parts[part * HEADS + group * 2]
            second = last_parts[part * HEADS + group * 2 + 1]
            feature = jnp.where(row == 3 + part, jnp.where(lane < BLOCK, first, second), feature)
    return feature.astype(bf16)


def turned(block):
    return block.astype(f32).T.astype(block.dtype)


def stacked_heads(pair):
    t = turned(pair)
    return jnp.concatenate([t[:HEAD_DIM], t[HEAD_DIM:]], axis=1)


def unstacked_heads(wide):
    return jnp.concatenate([wide[:, :BLOCK], wide[:, BLOCK:]], axis=0).T


def with_other(half, other, odd):
    return jnp.concatenate([other, half] if odd else [half, other], axis=0)


def fold_rows(tile):
    return tile.reshape(tile.shape[0] // 8, 8, tile.shape[1])


class Keys:
    def __init__(self, share, blocks, causal):
        self.share, self.blocks, self.causal = share, blocks, causal
        self.count = share * blocks

    def blocks_for(self, i):
        return (i + 1 if self.causal else self.blocks) * self.share

    def near(self, i, index, kinds):
        if not self.causal:
            return None
        j, s = divmod(index, self.share)
        kind = (s, i - j)
        return kinds.index(kind) if kind in kinds else None


def load_keys(keys, k_refs, feat_refs, odd, kaug):
    lane = lax.broadcasted_iota(jnp.int32, (BLOCK, 2 * HEAD_DIM), 1)
    own = (lane >= HEAD_DIM) if odd else (lane < HEAD_DIM)
    for index in range(keys.count):
        j, s = divmod(index, keys.share)
        rows = pl.ds(j * BLOCK, BLOCK)
        kaug[pl.ds(index * BLOCK, BLOCK), :] = jnp.where(
            own, k_refs[s][rows, :].astype(f32), feat_refs[s][rows, :].astype(f32)
        ).astype(bf16)


def turn_keys(keys, refs, target):
    for index in range(keys.count):
        j, s = divmod(index, keys.share)
        target[:, pl.ds(index * BLOCK, BLOCK)] = turned(refs[s][pl.ds(j * BLOCK, BLOCK), :])


def forward_kernel(keys, kinds, *refs):
    refs = list(refs)
    take = lambda n: [refs.pop(0) for _ in range(n)]
    q_ref, seg_ref = take(2)
    k_refs, v_refs, feat_refs = take(keys.share), take(keys.share), take(keys.share)
    tiles, last_parts = take(2) if keys.causal else (None, None)
    ctx_ref, log_ref, kaug, vt, sbuf, pbuf = refs
    pair = pl.program_id(0)
    turn_keys(keys, v_refs, vt)
    for gi in range(2):
        load_keys(keys, k_refs, feat_refs, gi, kaug)
        for i in range(q_ref.shape[0] // BLOCK):
            tokens = pl.ds(i * BLOCK, BLOCK)
            lanes = pl.ds(gi * BLOCK, BLOCK)
            features = query_features(seg_ref[:, tokens], last_parts, pair * 2 + gi)
            right = with_other(stacked_heads(q_ref[tokens, lanes]), features, gi)
            count = keys.blocks_for(i)
            top = jnp.full((8, 2 * BLOCK), -jnp.inf, f32)
            for index in range(count):
                rows = pl.ds(index * BLOCK, BLOCK)
                scores = nn(kaug[rows, :], right)
                near = keys.near(i, index, kinds)
                if near is not None:
                    scores = scores + tiles[gi, near]
                sbuf[rows, :] = scores
                top = jnp.maximum(top, jnp.max(fold_rows(scores), axis=0))
            top = jnp.max(top, axis=0, keepdims=True)
            total = jnp.zeros((8, 2 * BLOCK), f32)
            for index in range(count):
                rows = pl.ds(index * BLOCK, BLOCK)
                exponent = jnp.exp(sbuf[rows, :] - top)
                total = total + jnp.sum(fold_rows(exponent), axis=0)
                pbuf[rows, :] = exponent.astype(bf16)
            total = jnp.sum(total, axis=0, keepdims=True)
            length = count * BLOCK
            context = nn(vt[pl.ds(gi * HEAD_DIM, HEAD_DIM), :length], pbuf[:length, :])
            ctx_ref[tokens, lanes] = unstacked_heads(context * (1.0 / total)).astype(bf16)
            log_ref[gi, pl.ds(i, 1), :] = top + jnp.log(total)


def backward_kernel(keys, kinds, *refs):
    refs = list(refs)
    take = lambda n: [refs.pop(0) for _ in range(n)]
    q_ref, seg_ref = take(2)
    k_refs, v_refs, feat_refs = take(keys.share), take(keys.share), take(keys.share)
    tiles, last_parts = take(2) if keys.causal else (None, None)
    log_ref, dctx_ref = take(2)
    (dq_ref,) = take(1)
    dkv_refs = take(keys.share)
    dtiles, dfar = take(2) if keys.causal else (None, None)
    kaug, kt, vn, sbuf, pbuf, gbuf, dk_acc, dv_acc = refs
    pair = pl.program_id(0)
    turn_keys(keys, k_refs, kt)
    for index in range(keys.count):
        j, s = divmod(index, keys.share)
        vn[pl.ds(index * BLOCK, BLOCK), :] = v_refs[s][pl.ds(j * BLOCK, BLOCK), :]
    for gi in range(2):
        load_keys(keys, k_refs, feat_refs, gi, kaug)
        group_rows = pl.ds(gi * HEAD_DIM, HEAD_DIM)
        seen = set()
        far = jnp.zeros((8, 2 * BLOCK), f32)
        n_blocks = q_ref.shape[0] // BLOCK
        for i in reversed(range(n_blocks)):
            tokens = pl.ds(i * BLOCK, BLOCK)
            lanes = pl.ds(gi * BLOCK, BLOCK)
            features = query_features(seg_ref[:, tokens], last_parts, pair * 2 + gi)
            queries = stacked_heads(q_ref[tokens, lanes])
            right = with_other(queries, features, gi)
            grads = stacked_heads(dctx_ref[tokens, lanes])
            grads_right = with_other(grads, jnp.zeros_like(grads), gi)
            logsum = log_ref[gi, pl.ds(i, 1), :]
            count = keys.blocks_for(i)
            middle = jnp.zeros((8, 2 * BLOCK), f32)
            for index in range(count):
                rows = pl.ds(index * BLOCK, BLOCK)
                scores = nn(kaug[rows, :], right)
                near = keys.near(i, index, kinds)
                if near is not None:
                    scores = scores + tiles[gi, near]
                probs = jnp.exp(scores - logsum)
                grad_probs = nn(vn[rows, :], grads_right)
                middle = middle + jnp.sum(fold_rows(probs * grad_probs), axis=0)
                sbuf[rows, :] = probs
                gbuf[rows, :] = grad_probs
                pbuf[rows, :] = probs.astype(bf16)
            middle = jnp.sum(middle, axis=0, keepdims=True)
            length = count * BLOCK
            grad_v = nt(grads, pbuf[:length, :])
            for index in range(count):
                rows = pl.ds(index * BLOCK, BLOCK)
                grad_scores = (sbuf[rows, :] * (gbuf[rows, :] - middle)).astype(bf16)
                pbuf[rows, :] = grad_scores
                if keys.causal:
                    wide = grad_scores.astype(f32)
                    near = keys.near(i, index, kinds)
                    if near is None:
                        far = far + jnp.sum(fold_rows(wide), axis=0)
                    elif near in seen:
                        dtiles[gi, near] = dtiles[gi, near] + wide
                    else:
                        dtiles[gi, near] = wide
                        seen.add(near)
            grad_k = nt(queries, pbuf[:length, :])
            grad_q = nn(kt[group_rows, :length], pbuf[:length, :])
            dq_ref[tokens, lanes] = unstacked_heads(grad_q * SCALE).astype(bf16)
            if i == n_blocks - 1:
                dk_acc[group_rows, :length] = grad_k
                dv_acc[group_rows, :length] = grad_v
            else:
                dk_acc[group_rows, :length] += grad_k
                dv_acc[group_rows, :length] += grad_v
        if keys.causal:
            dfar[gi] = far
    for index in range(keys.count):
        j, s = divmod(index, keys.share)
        columns = pl.ds(index * BLOCK, BLOCK)
        rows = pl.ds(j * BLOCK, BLOCK)
        dkv_refs[s][0, rows, :] = dk_acc[:, columns].T.astype(bf16)
        dkv_refs[s][1, rows, :] = dv_acc[:, columns].T.astype(bf16)


def attention_operands(at, queries, key_values, features, seg_row, tiles, last_parts):
    causal = tiles is not None
    tokens = queries.shape[0]
    span = key_values[0].shape[0]
    keys = Keys(at.share, span // BLOCK, causal)
    operands = [queries, seg_row, *key_values, *key_values, *features]
    specs = [
        pl.BlockSpec((tokens, 2 * BLOCK), lambda p: (0, p)),
        pl.BlockSpec(seg_row.shape, lambda p: (0, 0)),
    ]
    specs += [pl.BlockSpec((span, BLOCK), lambda p: (0, p))] * at.share
    specs += [pl.BlockSpec((span, BLOCK), lambda p: (0, PAIRS + p))] * at.share
    specs += [pl.BlockSpec((span, BLOCK), lambda p: (0, 0))] * at.share
    if causal:
        operands += [tiles, last_parts]
        specs += [
            pl.BlockSpec((2, *tiles.shape[1:]), lambda p: (p, 0, 0, 0)),
            whole_smem(),
        ]
    return keys, operands, specs


def attention_forward(at, queries, key_values, features, seg_row, tiles=None, last_parts=None):
    keys, operands, specs = attention_operands(
        at, queries, key_values, features, seg_row, tiles, last_parts
    )
    tokens = queries.shape[0]
    blocks = tokens // BLOCK
    length = keys.count * BLOCK
    work = sum(keys.blocks_for(i) for i in range(blocks)) * BLOCK * 2 * BLOCK * GROUPS
    return pl.pallas_call(
        functools.partial(forward_kernel, keys, near_kinds(at.share)),
        grid=(PAIRS,),
        out_shape=[
            jax.ShapeDtypeStruct((tokens, HEADS * HEAD_DIM), bf16),
            jax.ShapeDtypeStruct((GROUPS, blocks, 2 * BLOCK), f32),
        ],
        in_specs=specs,
        out_specs=[
            pl.BlockSpec((tokens, 2 * BLOCK), lambda p: (0, p)),
            pl.BlockSpec((2, blocks, 2 * BLOCK), lambda p: (p, 0, 0)),
        ],
        scratch_shapes=[
            pltpu.VMEM((length, 2 * HEAD_DIM), bf16),
            pltpu.VMEM((2 * HEAD_DIM, length), bf16),
            pltpu.VMEM((length, 2 * BLOCK), f32),
            pltpu.VMEM((length, 2 * BLOCK), bf16),
        ],
        compiler_params=params(32),
        cost_estimate=pl.CostEstimate(
            flops=work * 512, bytes_accessed=8 * MIB, transcendentals=work
        ),
        name="self_forward" if keys.causal else "cross_forward",
    )(*operands)


def attention_backward(
    at, queries, key_values, features, seg_row, logsum, grad_context, tiles=None, last_parts=None
):
    keys, operands, specs = attention_operands(
        at, queries, key_values, features, seg_row, tiles, last_parts
    )
    tokens = queries.shape[0]
    span = key_values[0].shape[0]
    blocks = tokens // BLOCK
    length = keys.count * BLOCK
    work = sum(keys.blocks_for(i) for i in range(blocks)) * BLOCK * 2 * BLOCK * GROUPS
    operands += [logsum, grad_context]
    specs += [
        pl.BlockSpec((2, blocks, 2 * BLOCK), lambda p: (p, 0, 0)),
        pl.BlockSpec((tokens, 2 * BLOCK), lambda p: (0, p)),
    ]
    out_shape = [jax.ShapeDtypeStruct((tokens, HEADS * HEAD_DIM), bf16)]
    out_specs = [pl.BlockSpec((tokens, 2 * BLOCK), lambda p: (0, p))]
    out_shape += [jax.ShapeDtypeStruct((2, span, GROUPS * HEAD_DIM), bf16)] * at.share
    out_specs += [pl.BlockSpec((2, span, BLOCK), lambda p: (0, 0, p))] * at.share
    if keys.causal:
        out_shape += [
            jax.ShapeDtypeStruct(tiles.shape, f32),
            jax.ShapeDtypeStruct((GROUPS, 8, 2 * BLOCK), f32),
        ]
        out_specs += [
            pl.BlockSpec((2, *tiles.shape[1:]), lambda p: (p, 0, 0, 0)),
            pl.BlockSpec((2, 8, 2 * BLOCK), lambda p: (p, 0, 0)),
        ]
    return pl.pallas_call(
        functools.partial(backward_kernel, keys, near_kinds(at.share)),
        grid=(PAIRS,),
        out_shape=out_shape,
        in_specs=specs,
        out_specs=out_specs,
        scratch_shapes=[
            pltpu.VMEM((length, 2 * HEAD_DIM), bf16),
            pltpu.VMEM((2 * HEAD_DIM, length), bf16),
            pltpu.VMEM((length, 2 * HEAD_DIM), bf16),
            pltpu.VMEM((length, 2 * BLOCK), f32),
            pltpu.VMEM((length, 2 * BLOCK), bf16),
            pltpu.VMEM((length, 2 * BLOCK), f32),
            pltpu.VMEM((2 * HEAD_DIM, length), f32),
            pltpu.VMEM((2 * HEAD_DIM, length), f32),
        ],
        compiler_params=params(40),
        cost_estimate=pl.CostEstimate(
            flops=work * 1024, bytes_accessed=16 * MIB, transcendentals=work
        ),
        name="self_backward" if keys.causal else "cross_backward",
    )(*operands)


def gelu_parts(v):
    slope = math.sqrt(2 / math.pi)
    square = v * v
    t = jnp.tanh(slope * v * (1.0 + 0.044715 * square))
    half = 0.5 * (1.0 + t)
    derivative = half + 0.5 * v * (1.0 - t * t) * slope * (1.0 + 3 * 0.044715 * square)
    return v * half, derivative


def ffn_kernel(at, *refs):
    n_pieces = at.z_count * at.dp
    held_refs, cot_refs = refs[0:2], refs[2:4]
    pieces = refs[4 : 4 + n_pieces]
    out_refs = refs[4 + n_pieces : 8 + n_pieces]
    grad_refs = refs[8 + n_pieces : 12 + n_pieces]
    weights, acts, held, cot, out_stage, back_stage, in_sems, w_sems, out_sems = refs[
        12 + n_pieces :
    ]
    d = lax.axis_index("dp")
    tokens = held_refs[0].shape[0]
    width = pieces[0].shape[2]
    rows = pieces[0].shape[1]

    def columns(s):
        return pl.ds(pl.multiple_of(xor_static(d, s, at.dp) * width, width), width)

    loads = []
    for which, (sources, target) in enumerate(((held_refs, held), (cot_refs, cot))):
        for half in range(2):
            for s in range(at.dp):
                loads.append(
                    pltpu.make_async_copy(
                        sources[half].at[:, columns(s)],
                        target.at[pl.ds(half * tokens, tokens), pl.ds(s * width, width)],
                        in_sems.at[(which * 2 + half) * at.dp + s],
                    )
                )
    for k in range(at.z_count):
        for s in range(at.dp):
            number = k * at.dp + s
            loads.append(
                pltpu.make_async_copy(
                    pieces[number],
                    weights.at[:, pl.ds(k * rows, rows), pl.ds(s * width, width)],
                    w_sems.at[number],
                )
            )
    for copy in loads:
        copy.start()
    for copy in loads:
        copy.wait()

    tile = 256

    def step(index, carry):
        here = pl.ds(pl.multiple_of(index * tile, tile), tile)
        held_tile, cot_tile = held[here, :], cot[here, :]
        gate = nt(held_tile, weights[0])
        up = nt(held_tile, weights[1])
        grad_hidden = nt(cot_tile, weights[2])
        active, slope = gelu_parts(gate)
        hidden = (active * up).astype(bf16)
        acts[2, here, :] = hidden
        out_stage[here, :] = nn(hidden, weights[2]).astype(bf16)
        grad_gate = (grad_hidden * up * slope).astype(bf16)
        grad_up = (grad_hidden * active).astype(bf16)
        acts[0, here, :] = grad_gate
        acts[1, here, :] = grad_up
        back_stage[here, :] = (nn(grad_gate, weights[0]) + nn(grad_up, weights[1])).astype(bf16)
        return carry

    lax.fori_loop(0, 2 * tokens // tile, step, 0)

    stores = []
    for which, stage in enumerate((out_stage, back_stage)):
        for half in range(2):
            for s in range(at.dp):
                stores.append(
                    pltpu.make_async_copy(
                        stage.at[pl.ds(half * tokens, tokens), pl.ds(s * width, width)],
                        out_refs[which * 2 + half].at[:, columns(s)],
                        out_sems.at[(which * 2 + half) * at.dp + s],
                    )
                )
    for copy in stores:
        copy.start()

    hidden_rows = rows * at.z_count
    half_rows = hidden_rows // 2
    for start in range(0, hidden_rows, BLOCK):
        size = min(BLOCK, hidden_rows - start)
        for m in range(3):
            right = cot if m == 2 else held
            grad = tn(acts[m, :, start : start + size], right[...]).astype(bf16)
            low = max(0, min(size, half_rows - start))
            for part, (first, last) in enumerate(((0, low), (low, size))):
                if first == last:
                    continue
                order, _ = half_order(at.dp, part == 0)
                target = start + first - part * half_rows
                for place, s in enumerate(order):
                    sent, slot = divmod(place, at.dp // 2)
                    grad_refs[part * 2 + sent][
                        slot, m, target : target + last - first, :
                    ] = grad[first:last, s * width : (s + 1) * width]
    for copy in stores:
        copy.wait()


def ffn(at, held_own, held_other, cot_own, cot_other, pieces):
    tokens, features = held_own.shape
    rows, width = pieces[0].shape[1:]
    hidden = rows * at.z_count
    grad_shape = jax.ShapeDtypeStruct((at.dp // 2, 3, hidden // 2, width), bf16)
    token_shape = jax.ShapeDtypeStruct((tokens, features), bf16)
    return pl.pallas_call(
        functools.partial(ffn_kernel, at),
        out_shape=[token_shape] * 4 + [grad_shape] * 4,
        in_specs=[any_space()] * (4 + len(pieces)),
        out_specs=[any_space()] * 4 + [whole_vmem()] * 4,
        scratch_shapes=[
            pltpu.VMEM((3, hidden, features), bf16),
            pltpu.VMEM((3, 2 * tokens, hidden), bf16),
            pltpu.VMEM((2 * tokens, features), bf16),
            pltpu.VMEM((2 * tokens, features), bf16),
            pltpu.VMEM((2 * tokens, features), bf16),
            pltpu.VMEM((2 * tokens, features), bf16),
            pltpu.SemaphoreType.DMA((4 * at.dp,)),
            pltpu.SemaphoreType.DMA((len(pieces),)),
            pltpu.SemaphoreType.DMA((4 * at.dp,)),
        ],
        compiler_params=params(58),
        cost_estimate=pl.CostEstimate(
            flops=18 * 2 * tokens * features * hidden,
            bytes_accessed=40 * MIB,
            transcendentals=2 * tokens * hidden,
        ),
        name="ffn",
    )(held_own, held_other, cot_own, cot_other, *pieces)


def weight_grad_kernel(at, widths, *refs):
    n = len(widths)
    lefts, rights, outs = refs[:n], refs[n : 2 * n], refs[2 * n :]
    d = lax.axis_index("dp")
    core = lax.axis_index("tp") % 2
    rows = lefts[0].shape[1] // at.dp
    quarter = sum(widths) // 4
    for sent in range(2):
        half = core if sent == 0 else 1 - core
        offset = 0
        for left, right, total in zip(lefts, rights, widths):
            width = total // 2
            block = right[:, pl.ds(pl.multiple_of(half * width, width), width)]
            for s in range(at.dp):
                chosen = pl.ds(pl.multiple_of(xor_static(d, s, at.dp) * rows, rows), rows)
                grad = tn(left[:, chosen], block).astype(bf16)
                done = 0
                while done < width:
                    part, inside = divmod(offset + done, quarter)
                    take = min(width - done, quarter - inside)
                    order, _ = half_order(at.dp, part == 0)
                    outs[part * 2 + sent][order.index(s), :, inside : inside + take] = grad[
                        :, done : done + take
                    ]
                    done += take
            offset += width


def weight_grads(at, pairs):
    lefts = [left for left, _ in pairs]
    rights = [right for _, right in pairs]
    widths = [right.shape[1] for right in rights]
    features = lefts[0].shape[1]
    quarter = sum(widths) // 4
    shape = jax.ShapeDtypeStruct((at.dp, features // at.dp, quarter), bf16)
    low_keep, low_send, high_keep, high_send = pl.pallas_call(
        functools.partial(weight_grad_kernel, at, widths),
        out_shape=[shape] * 4,
        in_specs=[whole_vmem()] * (2 * len(pairs)),
        out_specs=[whole_vmem()] * 4,
        compiler_params=params(48),
        cost_estimate=pl.CostEstimate(
            flops=2 * lefts[0].shape[0] * features * sum(widths),
            bytes_accessed=16 * MIB,
            transcendentals=0,
        ),
        name="weight_grads",
    )(*lefts, *rights)
    core = lax.axis_index("tp") % 2
    mine = []
    for part, (keep, send) in enumerate(((low_keep, low_send), (high_keep, high_send))):
        received = lax.ppermute(send, "tp", at.core_perm())
        half = at.dp // 2
        keep, send = added(keep[:half], received[:half]), added(keep[half:], received[half:])
        total = reduce_dp(at, keep, send, part == 0)
        chunks = total.reshape(at.z_count, -1, quarter)
        z = lax.axis_index("tp") // 2
        result = lax.dynamic_index_in_dim(chunks, z, 0, keepdims=False).astype(f32)
        for k in range(1, at.z_count):
            chunk = lax.dynamic_index_in_dim(chunks, (z + k) % at.z_count, 0, keepdims=False)
            result = result + lax.ppermute(chunk, "tp", at.z_perm(k)).astype(f32)
        mine.append(result)
    joined = jnp.concatenate(mine, axis=1).astype(bf16)
    joined = joined.reshape(2, -1, joined.shape[-1])
    own = lax.dynamic_index_in_dim(joined, core, 0, keepdims=False)
    other = lax.ppermute(
        lax.dynamic_index_in_dim(joined, 1 - core, 0, keepdims=False), "tp", at.core_perm()
    )
    first = jnp.where(core == 0, own, other).astype(f32)
    second = jnp.where(core == 0, other, own).astype(f32)
    results, offset = [], 0
    for total in widths:
        inside = slice(offset, offset + total // 2)
        results.append(jnp.concatenate([first[:, inside], second[:, inside]], axis=1))
        offset += total // 2
    return results


def added(left, right):
    return (left.astype(f32) + right.astype(f32)).astype(bf16)


def reduce_dp(at, keep, send, first_low):
    _, bits = half_order(at.dp, first_low)
    for place, bit in enumerate(bits):
        received = lax.ppermute(send, "dp", at.dp_perm(1 << bit))
        half = keep.shape[0] // 2
        if half:
            keep, send = added(keep[:half], received[:half]), added(keep[half:], received[half:])
        else:
            return added(keep[0], received[0])


def reduce_ffn_grads(at, grads):
    low_keep, low_send, high_keep, high_send = grads
    low = reduce_dp(at, low_keep, low_send, True)
    high = reduce_dp(at, high_keep, high_send, False)
    half = at.z_count // 2
    chunks = []
    for total in (low, high):
        split = total.reshape(3, half, -1, total.shape[-1])
        chunks += [split[:, k] for k in range(half)]
    result = chunks[0].astype(f32)
    for k in range(1, at.z_count):
        result = result + lax.ppermute(chunks[k], "tp", at.z_perm(-k)).astype(f32)
    return result


def reduce_small(at, vector):
    core = lax.axis_index("tp") % 2
    z = lax.axis_index("tp") // 2
    d = lax.axis_index("dp")
    pick = lambda array, index: lax.dynamic_index_in_dim(array, index, 0, keepdims=False)
    array = vector.reshape(at.dp * at.z_count, 2, -1).transpose(1, 0, 2)
    array = pick(array, core) + lax.ppermute(pick(array, 1 - core), "tp", at.core_perm())
    array = array.reshape(at.dp, at.z_count, -1)
    total = pick(array, d)
    for s in range(1, at.dp):
        total = total + lax.ppermute(
            pick(array, xor_static(d, s, at.dp)), "dp", at.dp_perm(s)
        )
    result = pick(total, z)
    for k in range(1, at.z_count):
        result = result + lax.ppermute(
            pick(total, (z + k) % at.z_count), "tp", at.z_perm(k)
        )
    return result


def gather_ffn(at, own, after):
    pieces = []
    current = own
    for k in range(at.z_count):
        if k == 1:
            current, _ = lax.optimization_barrier((current, after))
        if k:
            current = lax.ppermute(current, "tp", at.z_perm(1))
        held = {0: current}
        _, bits = half_order(at.dp, k % 2 == 0)
        for bit in bits:
            for s in list(held):
                held[s | 1 << bit] = lax.ppermute(held[s], "dp", at.dp_perm(1 << bit))
        pieces += [held[s] for s in range(at.dp)]
    return pieces, current


def relative_grad(at, dtiles, dfar):
    kinds = near_kinds(at.share)
    onehots = []
    for kind in kinds:
        distance = tile_distance(at, kind)
        bucket = jnp.where(distance < 0, -1, bucket_of(jnp.maximum(distance, 0)))
        onehots.append(bucket[:, :, None] == jnp.arange(BUCKETS, dtype=jnp.int32))
    onehot = jnp.stack(onehots).astype(f32)
    tiles = dtiles.reshape(GROUPS, len(kinds), BLOCK, 2, BLOCK)
    near = jnp.einsum(
        "nkqb,gnkjq->bgj", onehot, tiles, precision=lax.Precision.HIGHEST
    ).reshape(BUCKETS, HEADS)
    far = jnp.sum(dfar.reshape(GROUPS, 8, 2, BLOCK), axis=(1, 3)).reshape(HEADS)
    return near.at[BUCKETS - 1].add(far)


def on_device(
    inputs,
    memory,
    segments,
    memory_segments,
    gain_self,
    gain_cross,
    gain_ffn,
    relative_bias,
    self_query,
    self_key,
    self_value,
    self_out,
    cross_query,
    cross_key,
    cross_value,
    cross_out,
    ffn_gate,
    ffn_up,
    ffn_down,
    cotangent,
):
    rows, seq, features = inputs.shape
    mem_seq = memory.shape[1]
    at = Places(rows)
    tokens = rows * seq
    mem_tokens = rows * mem_seq
    key_width = GROUPS * HEAD_DIM
    width = features // at.dp
    d = lax.axis_index("dp")

    x_pieces = exchange_rows(at, inputs)
    seg_parts = exchange_segments(at, jnp.concatenate([segments, memory_segments], axis=1))
    own_columns = lambda w: lax.dynamic_slice_in_dim(w, d * width, width, 1)
    own_rows = lambda w: lax.dynamic_slice_in_dim(w, d * width, width, 0).T
    own_piece = jnp.stack([own_rows(ffn_gate), own_rows(ffn_up), own_columns(ffn_down)])
    tiles = bias_tiles(at, relative_bias.reshape(-1))

    x_pieces, memory_in = lax.optimization_barrier((x_pieces, memory))
    mem_pieces = exchange_rows(at, memory_in)
    ffn_pieces, ring_end = gather_ffn(at, own_piece, mem_pieces)
    cot_in, _ = lax.optimization_barrier((cotangent, ring_end))
    cot_pieces = exchange_rows(at, cot_in)

    x = place_rows(at, inputs, x_pieces).reshape(tokens, features).astype(f32)

    last = relative_bias[BUCKETS - 1]
    high = lax.reduce_precision(last, 8, 7)
    mid = lax.reduce_precision(last - high, 8, 7)
    low = lax.reduce_precision(last - high - mid, 8, 7)
    last_parts = jnp.concatenate([high, mid, low])

    def key_features(seg):
        lane = jnp.arange(2 * HEAD_DIM, dtype=jnp.int32) % HEAD_DIM
        column = seg.reshape(-1, 1)
        return jnp.where(
            lane < 3, (column == lane).astype(f32), ((lane >= 3) & (lane < 6)).astype(f32)
        ).astype(bf16)

    self_features = [key_features(seg[:, :seq]) for seg in seg_parts]
    mem_features = [key_features(seg[:, seq:]) for seg in seg_parts]
    seg_row = seg_parts[0][:, :seq].reshape(1, tokens)

    held_self = (x * norm_scale(x) * gain_self).astype(bf16)
    queries = (nn(held_self, self_query) * SCALE).astype(bf16)
    kv = jnp.concatenate([nn(held_self, self_key), nn(held_self, self_value)], axis=1).astype(bf16)
    kvs = [kv] + [lax.ppermute(kv, "tp", at.part_perm(s)) for s in range(1, at.share)]
    mem = place_rows(at, memory, mem_pieces).reshape(mem_tokens, features)
    mem_kv = jnp.concatenate([nn(mem, cross_key), nn(mem, cross_value)], axis=1).astype(bf16)
    mem_kvs = [mem_kv] + [
        lax.ppermute(mem_kv, "tp", at.part_perm(s)) for s in range(1, at.share)
    ]
    self_context, self_log = attention_forward(
        at, queries, kvs, self_features, seg_row, tiles, last_parts
    )
    stream_one = x + nn(self_context, self_out)

    held_cross = (stream_one * norm_scale(stream_one) * gain_cross).astype(bf16)
    cross_queries = (nn(held_cross, cross_query) * SCALE).astype(bf16)
    cross_context, cross_log = attention_forward(
        at, cross_queries, mem_kvs, mem_features, seg_row
    )
    stream_two = stream_one + nn(cross_context, cross_out)

    held_ffn = (stream_two * norm_scale(stream_two) * gain_ffn).astype(bf16)
    cot = place_rows(at, cotangent, cot_pieces).reshape(tokens, features)
    cot_other = lax.ppermute(cot, "tp", at.core_perm())
    held_other = lax.ppermute(held_ffn, "tp", at.core_perm())
    out_own, out_other, back_own, back_other, *ffn_grads = ffn(
        at, held_ffn, held_other, cot, cot_other, ffn_pieces
    )
    back_received = lax.ppermute(back_other, "tp", at.core_perm())
    out_received = lax.ppermute(out_other, "tp", at.core_perm())
    ffn_sum = reduce_ffn_grads(at, ffn_grads)

    grad_held = back_own.astype(f32) + back_received.astype(f32)
    grad_stream, gain_ffn_part = norm_back(stream_two, gain_ffn, grad_held)
    grad_two = cot.astype(f32) + grad_stream
    output = (stream_two + (out_own.astype(f32) + out_received.astype(f32))).astype(bf16)
    output = output.reshape(rows, seq, features)
    output_pieces = exchange_rows(at, output)

    cross_branch = grad_two.astype(bf16)
    grad_cross_context = nt(cross_branch, cross_out).astype(bf16)
    grad_cross_queries, *grad_mem_kvs = attention_backward(
        at, cross_queries, mem_kvs, mem_features, seg_row, cross_log, grad_cross_context
    )

    def gathered_grads(parts):
        total = parts[0].astype(f32)
        for s in range(1, at.share):
            total = total + lax.ppermute(
                parts[s], "tp", at.part_perm(at.share - s)
            ).astype(f32)
        return total[0].astype(bf16), total[1].astype(bf16)

    grad_mem_keys, grad_mem_values = gathered_grads(grad_mem_kvs)
    grad_stream, gain_cross_part = norm_back(
        stream_one, gain_cross, nt(grad_cross_queries, cross_query)
    )
    grad_one = grad_two + grad_stream
    self_branch = grad_one.astype(bf16)
    grad_self_context = nt(self_branch, self_out).astype(bf16)
    memory_grad = (nt(grad_mem_keys, cross_key) + nt(grad_mem_values, cross_value)).astype(bf16)
    memory_grad = memory_grad.reshape(rows, mem_seq, features)
    memory_pieces = exchange_rows(at, memory_grad)
    cross_out_grad, cross_query_grad, self_out_grad, cross_key_grad, cross_value_grad = (
        weight_grads(
            at,
            [
                (cross_context, cross_branch),
                (held_cross, grad_cross_queries),
                (self_context, self_branch),
                (mem, grad_mem_keys),
                (mem, grad_mem_values),
            ],
        )
    )

    grad_queries, *more = attention_backward(
        at, queries, kvs, self_features, seg_row, self_log, grad_self_context, tiles, last_parts
    )
    grad_keys, grad_values = gathered_grads(more[: at.share])
    self_query_grad, self_key_grad, self_value_grad = weight_grads(
        at, [(held_self, grad_queries), (held_self, grad_keys), (held_self, grad_values)]
    )
    grad_stream, gain_self_part = norm_back(
        x,
        gain_self,
        nt(grad_queries, self_query) + nt(grad_keys, self_key) + nt(grad_values, self_value),
    )
    input_grad = (grad_one + grad_stream).astype(bf16).reshape(rows, seq, features)
    input_pieces = exchange_rows(at, input_grad)
    relative_part = relative_grad(at, more[at.share], more[at.share + 1])

    shards = at.dp * at.tp
    small = jnp.concatenate(
        [
            part.reshape(shards, -1)
            for part in (gain_self_part, gain_cross_part, gain_ffn_part, relative_part)
        ],
        axis=1,
    )
    small = reduce_small(at, small)
    g = features // shards
    return (
        place_rows(at, output, output_pieces),
        place_wide(at, input_grad, input_pieces),
        place_wide(at, memory_grad, memory_pieces),
        small[:g],
        small[g : 2 * g],
        small[2 * g : 3 * g],
        small[3 * g :],
        self_query_grad,
        self_key_grad,
        self_value_grad,
        self_out_grad,
        cross_query_grad,
        cross_key_grad,
        cross_value_grad,
        cross_out_grad,
        ffn_sum[0].T,
        ffn_sum[1].T,
        ffn_sum[2],
    )


def solution(mesh):
    placed = (
        P("dp", "tp", None),
        P("dp", "tp", None),
        P("dp", "tp"),
        P("dp", "tp"),
        P(),
        P(),
        P(),
        P(),
        P(),
        P(),
        P(),
        P(),
        P(),
        P(),
        P(),
        P(),
        P(None, "tp"),
        P(None, "tp"),
        P("tp", None),
        P("dp", "tp", None),
    )
    return jax.shard_map(
        on_device,
        mesh=mesh,
        in_specs=placed,
        out_specs=(
            P("dp", "tp", None),
            P("dp", "tp", None),
            P("dp", "tp", None),
            P(("dp", "tp")),
            P(("dp", "tp")),
            P(("dp", "tp")),
            P(("dp", "tp")),
            P(("dp", "tp"), None),
            P(("dp", "tp"), None),
            P(("dp", "tp"), None),
            P(("dp", "tp"), None),
            P(("dp", "tp"), None),
            P(("dp", "tp"), None),
            P(("dp", "tp"), None),
            P(("dp", "tp"), None),
            P("dp", "tp"),
            P("dp", "tp"),
            P("tp", "dp"),
        ),
        check_vma=False,
    )
```

time: 1970 us -> 648 us (0.33)
  waiting for transfers between devices: 1190 us -> 163 us
  matrix products: 393 us -> 30.4 us
  Pallas kernels: 0 us -> 248 us
  local copies, waits for them, and re-layouts: 226 us -> 29.8 us
  starting transfers between devices: 1.6 us -> 118 us
  blocking collectives: 67.7 us -> 0 us
    reduce_scatter x14 -> x0, waiting for transfers between devices: 884 us -> none  [the longest x1 143 us: on_device(): lax.psum_scatter(self_out_part, ('dp', 'tp'), scatter_dimension=0, tiled=...]
    dot_general x147 -> x17, matrix products: 393 us -> 30.4 us  [the longest x8 12.7 us: nt(): lax.dot_general(left, right, (((1,), (1,)), ((), ())), preferred_element_...]
    unnamed x23 -> x0, waiting for transfers between devices: 276 us -> none
    pallas_call x0 -> x14, Pallas kernels: none -> 248 us  [the longest x4 116 us: place_rows(): pl.pallas_call(functools.partial(place_kernel, at), out_shape=jax.ShapeDt...]
    ppermute x0 -> x85, waiting for transfers between devices: none -> 163 us  [the longest x21 33.2 us: exchange_rows(): received.append(lax.ppermute(chunk, 'tp', at.row_perm(k)))]
    ppermute x0 -> x85, starting transfers between devices: none -> 118 us  [the longest x21 37.9 us: exchange_rows(): received.append(lax.ppermute(chunk, 'tp', at.row_perm(k)))]
    eq x1 -> x4, local copies, waits for them, and re-layouts: 74.9 us -> 0.17 us  [key_features(): column == lane]
    unnamed x1 -> x0, blocking collectives: 40.3 us -> none
  transfers between devices with their start and end apart: 21 -> 85, of which waited for: 12 -> 28; matrix products, arithmetic and copies ran while one was open for 33% -> 14% of each run, Pallas kernels for 0% -> 33%
where the time goes in v1:
time: 648 us; the launch traced here: 639 us
  Pallas kernels  248 us (38%)
  waiting for transfers between devices  163 us (25%)
  starting transfers between devices  118 us (18%)
  other arithmetic  46.8 us (7%)
  matrix products  30.4 us (5%)
  local copies, waits for them, and re-layouts  29.8 us (5%)
    pallas_call x4, Pallas kernels, place_rows(): pl.pallas_call(functools.partial(place_kernel, at), out_shape=jax.ShapeDt...  116 us
    pallas_call x1, Pallas kernels, ffn(): pl.pallas_call(functools.partial(ffn_kernel, at), out_shape=[token_shape]...  39.5 us
    pallas_call x2, Pallas kernels, attention_backward(): pl.pallas_call(functools.partial(backward_kernel, keys, near_kinds(at.sha...  38.6 us
    ppermute x21, starting transfers between devices, exchange_rows(): received.append(lax.ppermute(chunk, 'tp', at.row_perm(k)))  37.9 us
    ppermute x21, waiting for transfers between devices, exchange_rows(): received.append(lax.ppermute(chunk, 'tp', at.row_perm(k)))  33.2 us
    ppermute x12, waiting for transfers between devices, reduce_dp(): received = lax.ppermute(send, 'dp', at.dp_perm(1 << bit))  32.8 us
    ppermute x12, starting transfers between devices, weight_grads(): result = result + lax.ppermute(chunk, 'tp', at.z_perm(k)).astype(f32)  30.8 us
    ppermute x3, waiting for transfers between devices, reduce_small(): lax.ppermute(pick(array, xor_static(d, s, at.dp)), 'dp', at.dp_perm(s))  28.8 us
  transfers between devices with their start and end apart: 85, of which 28 were waited for; matrix products, arithmetic and copies ran while one was open for 14% of the time, Pallas kernels for 33%

profile of v1, /device:TPU:0, one launch (start us, length us, event | category | flops | bytes accessed | tf_op | source)
XLA Modules:
  0.0 639.4 jit_solution(15187847500727758975)
XLA Ops:
  18.2 11.1 %bias_tiles.1.refs_8_ = f32[8,3,128,256]{3,2,1,0:T(8,128)} custom-call(f32[512]{0:T(512)} %reshape.486.table), custom_call_target="tpu_custom_call" | custom-call | tf_op jit(solution)/shard_map/bias_tiles/pallas_call | solution.py:237
  33.6 4.3 collective-permute-done.2.refs_3_
  38.0 32.9 %place_rows.4 = bf16[4,128,1024]{2,1,0:T(8,128)(2,1)} custom-call(bf16[4,128,1024]{2,1,0:T(8,128)(2,1)} %refs_0_.3, bf16[128,1024]{1,0:T(8,128)(2,1)} %copy-done.64, bf16[128,1024]{1,0:T(8,128)(2,1)} %collective-permute-done.1.refs_2_, bf16[128,1024]{1,0:T(8,128)(2,1)} %collective-permute-done.2.refs_3_), custom_call_target="tpu_custom_call" | custom-call | tf_op jit(solution)/shard_map/place_rows/pallas_call | solution.py:161
  89.0 5.8 collective-permute-done.9.refs_2_
  98.1 17.0 %place_rows.5 = bf16[4,64,1024]{2,1,0:T(8,128)(2,1)} custom-call(bf16[4,64,1024]{2,1,0:T(8,128)(2,1)} %refs_0_.4, bf16[64,1024]{1,0:T(8,128)(2,1)} %copy-done.68, bf16[64,1024]{1,0:T(8,128)(2,1)} %copy-done.69, bf16[64,1024]{1,0:T(8,128)(2,1)} %copy-done.70), custom_call_target="tpu_custom_call" | custom-call | tf_op jit(solution)/shard_map/place_rows/pallas_call | solution.py:161
  121.8 14.8 %self_forward.1 = (bf16[512,1024]{1,0:T(8,128)(2,1)S(1)}, f32[8,4,256]{2,1,0:T(4,128)S(1)}) custom-call(bf16[512,1024]{1,0:T(8,128)(2,1)S(1)} %copy-done.24, s32[1,512]{1,0:T(1,128)S(1)} %bitcast.282, bf16[512,1024]{1,0:T(8,128)(2,1)S(1)} %pad_maximum_fusion.refs_2_.refs_4_, bf16[512,1024]{1,0:T(8,128)(2,1)} %collective-permute-done.6.refs_3_.refs_5_, ...), custom_call_target="tpu_custom_call" | custom-call | flops 2684354560 | bytes 8388608 | tf_op jit(solution)/shard_map/self_forward/pallas_call | solution.py:466
  141.6 12.7 %cross_forward.1 = (bf16[512,1024]{1,0:T(8,128)(2,1)S(1)}, f32[8,4,256]{2,1,0:T(4,128)S(1)}) custom-call(bf16[512,1024]{1,0:T(8,128)(2,1)S(1)} %multiply_convert_fusion.1.refs_0_, s32[1,512]{1,0:T(1,128)S(1)} %bitcast.283, bf16[256,1024]{1,0:T(8,128)(2,1)S(1)} %pad_maximum_fusion.2.refs_2_.refs_4_, ...), custom_call_target="tpu_custom_call" | custom-call | flops 2147483648 | bytes 8388608 | tf_op jit(solution)/shard_map/cross_forward/pallas_call | solution.py:466
  169.6 7.0 %collective-permute-done.17.refs_2_ = bf16[128,1024]{1,0:T(8,128)(2,1)S(1)} collective-permute-done((bf16[128,1024]{1,0:T(8,128)(2,1)S(1)}, bf16[128,1024]{1,0:T(8,128)(2,1)S(1)}, u32[]{:S(2)}, u32[]{:S(2)}) %collective-permute-start.17) | collective-permute-done | bytes 262176 | tf_op jit(solution)/shard_map/ppermute | solution.py:140
  180.9 32.9 %place_rows.6 = bf16[4,128,1024]{2,1,0:T(8,128)(2,1)} custom-call(bf16[4,128,1024]{2,1,0:T(8,128)(2,1)} %refs_0_.5, bf16[128,1024]{1,0:T(8,128)(2,1)} %copy-done.65, bf16[128,1024]{1,0:T(8,128)(2,1)} %copy-done.66, bf16[128,1024]{1,0:T(8,128)(2,1)} %copy-done.67), custom_call_target="tpu_custom_call" | custom-call | tf_op jit(solution)/shard_map/place_rows/pallas_call | solution.py:161
  218.2 12.0 %collective-permute-done.28.refs_15_ = bf16[3,352,256]{2,1,0:T(8,128)(2,1)} collective-permute-done((bf16[3,352,256]{2,1,0:T(8,128)(2,1)}, bf16[3,352,256]{2,1,0:T(8,128)(2,1)}, u32[]{:S(2)}, u32[]{:S(2)}) %collective-permute-start.28) | collective-permute-done | bytes 540704 | tf_op jit(solution)/shard_map/ppermute | solution.py:827
  230.1 10.4 %collective-permute-done.31.refs_19_ = bf16[3,352,256]{2,1,0:T(8,128)(2,1)} collective-permute-done((bf16[3,352,256]{2,1,0:T(8,128)(2,1)}, bf16[3,352,256]{2,1,0:T(8,128)(2,1)}, u32[]{:S(2)}, u32[]{:S(2)}) %collective-permute-start.31) | collective-permute-done | bytes 540704 | tf_op jit(solution)/shard_map/ppermute | solution.py:827
  240.5 39.5 %ffn.1 = (bf16[512,1024]{1,0:T(8,128)(2,1)}, bf16[512,1024]{1,0:T(8,128)(2,1)}, bf16[512,1024]{1,0:T(8,128)(2,1)}, bf16[512,1024]{1,0:T(8,128)(2,1)}, bf16[2,3,7...) custom-call(bf16[512,1024]{1,0:T(8,128)(2,1)} %copy-done.60, ...), custom_call_target="tpu_custom_call" | custom-call | flops 26575110144 | bytes 41943040 | tf_op jit(solution)/shard_map/ffn/pallas_call | solution.py:660
  295.0 17.5 %cross_backward.1 = (bf16[512,1024]{1,0:T(8,128)(2,1)S(1)}, bf16[2,256,512]{2,1,0:T(8,128)(2,1)S(1)}, bf16[2,256,512]{2,1,0:T(8,128)(2,1)}) custom-call(bf16[512,1024]{1,0:T(8,128)(2,1)S(1)} %copy-done.31, s32[1,512]{1,0:T(1,128)S(1)} %bitcast.284, bf16[256,1024]{1,0:T(8,128)(2,1)S(1)} %copy-done.16, bf16[256,1024]{1,0:T(8,128)(2,1)S(1)} %copy-done.20, ...), custom_call_target="tpu_custom_call" | custom-call | flops 4294967296 | bytes 16777216 | tf_op jit(solution)/shard_map/cross_backward/pallas_call | solution.py:521
  314.7 4.3 fusion.118
  328.7 21.0 %self_backward.1 = (bf16[512,1024]{1,0:T(8,128)(2,1)S(1)}, bf16[2,512,512]{2,1,0:T(8,128)(2,1)S(1)}, bf16[2,512,512]{2,1,0:T(8,128)(2,1)S(1)}, f32[8,3,128,256]{3,2,1,0:T(8,128)S(1)}, f32[8,8,256]{2,1,0:T(8,128)S(1)}) custom-call(bf16[512,1024]{1,0:T(8,128)(2,1)S(1)} %copy-done.25, s32[1,512]{1,0:T(1,128)S(1)} %bitcast.285, ...), custom_call_target="tpu_custom_call" | custom-call | flops 5368709120 | bytes 16777216 | tf_op jit(solution)/shard_map/self_backward/pallas_call | solution.py:521
  355.9 4.8 copy.60
  360.9 4.9 fusion.17
  366.5 4.3 fusion.127
  371.0 32.9 %place_rows.7 = bf16[4,128,1024]{2,1,0:T(8,128)(2,1)} custom-call(bf16[4,128,1024]{2,1,0:T(8,128)(2,1)} %bitcast.290, bf16[128,1024]{1,0:T(8,128)(2,1)} %collective-permute-done.33.refs_1_, bf16[128,1024]{1,0:T(8,128)(2,1)} %collective-permute-done.34.refs_2_, bf16[128,1024]{1,0:T(8,128)(2,1)} %collective-permute-done.35.refs_3_), custom_call_target="tpu_custom_call" | custom-call | tf_op jit(solution)/shard_map/place_rows/pallas_call | solution.py:161
  410.8 8.7 %weight_grads.3 = (bf16[4,256,1024]{2,1,0:T(8,128)(2,1)}, bf16[4,256,1024]{2,1,0:T(8,128)(2,1)}, bf16[4,256,1024]{2,1,0:T(8,128)(2,1)}, bf16[4,256,1024]{2,1,0:T(8,128)(2,1)}) custom-call(bf16[512,1024]{1,0:T(8,128)(2,1)S(1)} %copy-done.27, bf16[512,1024]{1,0:T(8,128)(2,1)S(1)} %copy-done.8, bf16[512,1024]{1,0:T(8,128)(2,1)S(1)} %copy-done.23, ...), custom_call_target="tpu_custom_call" | custom-call | flops 4294967296 | bytes 16777216 | tf_op jit(solution)/shard_map/weight_grads/pallas_call | solution.py:721
  434.9 4.8 weight_grads.2
  439.7 28.8 %collective-permute-done.48 = f32[4,112]{1,0:T(4,128)S(1)} collective-permute-done((f32[4,112]{1,0:T(4,128)S(1)}, f32[4,112]{1,0:T(4,128)S(1)}, u32[]{:S(2)}, u32[]{:S(2)}) %collective-permute-start.48) | collective-permute-done | bytes 1824 | tf_op jit(solution)/shard_map/ppermute | solution.py:804
  484.3 4.5 collective-permute-done.39.refs_2_
  491.1 6.0 collective-permute-done.40.refs_3_
  501.8 5.6 collective-permute-done.82
  509.9 15.4 %collective-permute-done.79 = bf16[1,3,704,256]{3,2,1,0:T(8,128)(2,1)S(1)} collective-permute-done((bf16[1,3,704,256]{3,2,1,0:T(8,128)(2,1)S(1)}, bf16[1,3,704,256]{3,2,1,0:T(8,128)(2,1)S(1)}, u32[]{:S(2)}, u32[]{:S(2)}) %collective-permute-start.79) | collective-permute-done | bytes 1081376 | tf_op jit(solution)/shard_map/ppermute | solution.py:771
  543.9 20.0 %collective-permute-done.83 = bf16[3,352,256]{2,1,0:T(8,128)(2,1)S(1)} collective-permute-done((bf16[3,352,256]{2,1,0:T(8,128)(2,1)S(1)}, bf16[3,352,256]{2,1,0:T(8,128)(2,1)S(1)}, u32[]{:S(2)}, u32[]{:S(2)}) %collective-permute-start.83) | collective-permute-done | bytes 540704 | tf_op jit(solution)/shard_map/ppermute | solution.py:790
  565.4 14.1 %collective-permute-start.57 = (bf16[64,512]{1,0:T(8,128)(2,1)S(1)}, bf16[64,512]{1,0:T(8,128)(2,1)S(1)}, u32[]{:S(2)}, u32[]{:S(2)}) collective-permute-start(bf16[64,512]{1,0:T(8,128)(2,1)S(1)} %get-tuple-element.164), channel_id=1, source_target_pairs={{0,6},{1,7},{2,0},{3,1},{4,2},{5,3},{6,4},{7,5},{8,14},{9,15},{10,... | collective-permute-start | bytes 196616 | tf_op jit(solution)/shard_map/ppermute | solution.py:746
  581.4 4.2 collective-permute-start.63
  597.6 10.6 %collective-permute-done.67 = bf16[1,256,1024]{2,1,0:T(8,128)(2,1)S(1)} collective-permute-done((bf16[1,256,1024]{2,1,0:T(8,128)(2,1)S(1)}, bf16[1,256,1024]{2,1,0:T(8,128)(2,1)S(1)}, u32[]{:S(2)}, u32[]{:S(2)}) %collective-permute-start.67) | collective-permute-done | bytes 524320 | tf_op jit(solution)/shard_map/ppermute | solution.py:771
  608.5 4.7 collective-permute-start.70
  620.2 9.6 %collective-permute-done.69 = bf16[64,1024]{1,0:T(8,128)(2,1)S(1)} collective-permute-done((bf16[64,1024]{1,0:T(8,128)(2,1)S(1)}, bf16[64,1024]{1,0:T(8,128)(2,1)S(1)}, u32[]{:S(2)}, u32[]{:S(2)}) %collective-permute-start.69) | collective-permute-done | bytes 131104 | tf_op jit(solution)/shard_map/ppermute | solution.py:746
  (499 shorter events, 209.1 us)
Async XLA Ops:
  2.1 31.5 %collective-permute-start = (bf16[128,1024]{1,0:T(8,128)(2,1)S(1)}, bf16[128,1024]{1,0:T(8,128)(2,1)S(1)}, u32[]{:S(2)}, u32[]{:S(2)}) collective-permute-start(bf16[128,1024]{1,0:T(8,128)(2,1)S(1)} %get-tuple-element.133), channel_id=1, source_target_pairs={{0,2},{1,3},{2,0},{3,1},{4,6},{5,7},{6,4},{7,5},{8,10},{9,11},{10,... | collective-permute-start | bytes 786440 | tf_op jit(solution)/shard_map/ppermute | solution.py:140
  29.4 89.7 %collective-permute-start.20 = (bf16[3,352,256]{2,1,0:T(8,128)(2,1)}, bf16[3,352,256]{2,1,0:T(8,128)(2,1)}, u32[]{:S(2)}, u32[]{:S(2)}) collective-permute-start(bf16[3,352,256]{2,1,0:T(8,128)(2,1)} %pad_maximum_fusion.1.refs_4_), channel_id=1, source_target_pairs={{0,8},{8,0},{16,24},{24,16},{1,9},{9,1},{17,25},{25,17},{2,10},{10... | collective-permute-start | bytes 1622024 | tf_op jit(solution)/shard_map/ppermute | solution.py:827
  77.7 43.6 %collective-permute-start.6 = (bf16[512,1024]{1,0:T(8,128)(2,1)S(1)}, bf16[512,1024]{1,0:T(8,128)(2,1)}, u32[]{:S(2)}, u32[]{:S(2)}) collective-permute-start(bf16[512,1024]{1,0:T(8,128)(2,1)S(1)} %pad_maximum_fusion.refs_2_.refs_4_), channel_id=1, source_target_pairs={{1,0},{0,1},{3,2},{2,3},{5,4},{4,5},{7,6},{6,7},{9,8},{8,9},{11,10... | collective-permute-start | bytes 3145736 | tf_op jit(solution)/shard_map/ppermute | solution.py:914
  87.5 70.0 %collective-permute-start.21 = (bf16[3,352,256]{2,1,0:T(8,128)(2,1)}, bf16[3,352,256]{2,1,0:T(8,128)(2,1)}, u32[]{:S(2)}, u32[]{:S(2)}) collective-permute-start(bf16[3,352,256]{2,1,0:T(8,128)(2,1)} %pad_maximum_fusion.1.refs_4_), channel_id=1, source_target_pairs={{0,16},{8,24},{16,0},{24,8},{1,17},{9,25},{17,1},{25,9},{2,18},{10... | collective-permute-start | bytes 1622024 | tf_op jit(solution)/shard_map/ppermute | solution.py:827
  119.1 43.0 %collective-permute-start.22 = (bf16[3,352,256]{2,1,0:T(8,128)(2,1)}, bf16[3,352,256]{2,1,0:T(8,128)(2,1)S(1)}, u32[]{:S(2)}, u32[]{:S(2)}) collective-permute-start(bf16[3,352,256]{2,1,0:T(8,128)(2,1)} %collective-permute-done.20.refs_5_), channel_id=1, source_target_pairs={{0,16},{8,24},{16,0},{24,8},{1,17},{9,25},{17,1},{25,9},{2,18},{10... | collective-permute-start | bytes 1622024 | tf_op jit(solution)/shard_map/ppermute | solution.py:827
  121.3 33.1 %collective-permute-start.24 = (bf16[3,352,256]{2,1,0:T(8,128)(2,1)}, bf16[3,352,256]{2,1,0:T(8,128)(2,1)}, u32[]{:S(2)}, u32[]{:S(2)}) collective-permute-start(bf16[3,352,256]{2,1,0:T(8,128)(2,1)} %collective-permute-done.13.refs_8_), channel_id=1, source_target_pairs={{0,16},{8,24},{16,0},{24,8},{1,17},{9,25},{17,1},{25,9},{2,18},{10... | collective-permute-start | bytes 1622024 | tf_op jit(solution)/shard_map/ppermute | solution.py:827
  154.4 59.4 %collective-permute-start.25 = (bf16[3,352,256]{2,1,0:T(8,128)(2,1)}, bf16[3,352,256]{2,1,0:T(8,128)(2,1)}, u32[]{:S(2)}, u32[]{:S(2)}) collective-permute-start(bf16[3,352,256]{2,1,0:T(8,128)(2,1)} %collective-permute-done.24.refs_10_), channel_id=1, source_target_pairs={{0,8},{8,0},{16,24},{24,16},{1,9},{9,1},{17,25},{25,17},{2,10},{10... | collective-permute-start | bytes 1622024 | tf_op jit(solution)/shard_map/ppermute | solution.py:827
  162.1 52.2 %collective-permute-start.26 = (bf16[3,352,256]{2,1,0:T(8,128)(2,1)}, bf16[3,352,256]{2,1,0:T(8,128)(2,1)}, u32[]{:S(2)}, u32[]{:S(2)}) collective-permute-start(bf16[3,352,256]{2,1,0:T(8,128)(2,1)} %collective-permute-done.14.refs_12_), channel_id=1, source_target_pairs={{0,8},{8,0},{16,24},{24,16},{1,9},{9,1},{17,25},{25,17},{2,10},{10... | collective-permute-start | bytes 1622024 | tf_op jit(solution)/shard_map/ppermute | solution.py:827
  163.7 52.2 %collective-permute-start.27 = (bf16[3,352,256]{2,1,0:T(8,128)(2,1)}, bf16[3,352,256]{2,1,0:T(8,128)(2,1)}, u32[]{:S(2)}, u32[]{:S(2)}) collective-permute-start(bf16[3,352,256]{2,1,0:T(8,128)(2,1)} %collective-permute-done.14.refs_12_), channel_id=1, source_target_pairs={{0,16},{8,24},{16,0},{24,8},{1,17},{9,25},{17,1},{25,9},{2,18},{10... | collective-permute-start | bytes 1622024 | tf_op jit(solution)/shard_map/ppermute | solution.py:827
  176.6 39.7 %collective-permute-start.30 = (bf16[3,352,256]{2,1,0:T(8,128)(2,1)}, bf16[3,352,256]{2,1,0:T(8,128)(2,1)}, u32[]{:S(2)}, u32[]{:S(2)}) collective-permute-start(bf16[3,352,256]{2,1,0:T(8,128)(2,1)} %collective-permute-done.15.refs_16_), channel_id=1, source_target_pairs={{0,16},{8,24},{16,0},{24,8},{1,17},{9,25},{17,1},{25,9},{2,18},{10... | collective-permute-start | bytes 1622024 | tf_op jit(solution)/shard_map/ppermute | solution.py:827
  180.8 37.3 %collective-permute-start.12 = (bf16[512,1024]{1,0:T(8,128)(2,1)S(1)}, bf16[512,1024]{1,0:T(8,128)(2,1)}, u32[]{:S(2)}, u32[]{:S(2)}) collective-permute-start(bf16[512,1024]{1,0:T(8,128)(2,1)S(1)} %multiply_convert_fusion.refs_0_), channel_id=1, source_target_pairs={{0,1},{1,0},{2,3},{3,2},{4,5},{5,4},{6,7},{7,6},{8,9},{9,8},{10,11... | collective-permute-start | bytes 3145736 | tf_op jit(solution)/shard_map/ppermute | solution.py:935
  285.7 28.6 %collective-permute-start.32 = (bf16[512,1024]{1,0:T(8,128)(2,1)}, bf16[512,1024]{1,0:T(8,128)(2,1)S(1)}, u32[]{:S(2)}, u32[]{:S(2)}) collective-permute-start(bf16[512,1024]{1,0:T(8,128)(2,1)} %get-tuple-element.73), channel_id=1, source_target_pairs={{0,1},{1,0},{2,3},{3,2},{4,5},{5,4},{6,7},{7,6},{8,9},{9,8},{10,11... | collective-permute-start | bytes 3145736 | tf_op jit(solution)/shard_map/ppermute | solution.py:940
  286.2 192.5 %collective-permute-start.81 = (bf16[2,3,704,256]{3,2,1,0:T(8,128)(2,1)}, bf16[2,3,704,256]{3,2,1,0:T(8,128)(2,1)}, u32[]{:S(2)}, u32[]{:S(2)}) collective-permute-start(bf16[2,3,704,256]{3,2,1,0:T(8,128)(2,1)} %get-tuple-element.97), channel_id=1, source_target_pairs={{0,16},{8,24},{16,0},{24,8},{1,17},{9,25},{17,1},{25,9},{2,18},{10... | collective-permute-start | bytes 6488072 | tf_op jit(solution)/shard_map/ppermute | solution.py:771
  320.0 50.9 %collective-permute-start.33 = (bf16[128,1024]{1,0:T(8,128)(2,1)}, bf16[128,1024]{1,0:T(8,128)(2,1)}, u32[]{:S(2)}, u32[]{:S(2)}) collective-permute-start(bf16[128,1024]{1,0:T(8,128)(2,1)} %get-tuple-element.127), channel_id=1, source_target_pairs={{0,2},{1,3},{2,0},{3,1},{4,6},{5,7},{6,4},{7,5},{8,10},{9,11},{10,... | collective-permute-start | bytes 786440 | tf_op jit(solution)/shard_map/ppermute | solution.py:140
  323.4 47.6 %collective-permute-start.34 = (bf16[128,1024]{1,0:T(8,128)(2,1)}, bf16[128,1024]{1,0:T(8,128)(2,1)}, u32[]{:S(2)}, u32[]{:S(2)}) collective-permute-start(bf16[128,1024]{1,0:T(8,128)(2,1)} %get-tuple-element.126), channel_id=1, source_target_pairs={{0,4},{1,5},{2,6},{3,7},{4,0},{5,1},{6,2},{7,3},{8,12},{9,13},{10,... | collective-permute-start | bytes 786440 | tf_op jit(solution)/shard_map/ppermute | solution.py:140
  325.1 45.9 %collective-permute-start.35 = (bf16[128,1024]{1,0:T(8,128)(2,1)}, bf16[128,1024]{1,0:T(8,128)(2,1)}, u32[]{:S(2)}, u32[]{:S(2)}) collective-permute-start(bf16[128,1024]{1,0:T(8,128)(2,1)} %get-tuple-element.125), channel_id=1, source_target_pairs={{0,6},{1,7},{2,4},{3,5},{4,2},{5,3},{6,0},{7,1},{8,14},{9,15},{10,... | collective-permute-start | bytes 786440 | tf_op jit(solution)/shard_map/ppermute | solution.py:140
  327.6 76.3 %collective-permute-start.41 = (bf16[2,256,512]{2,1,0:T(8,128)(2,1)}, bf16[2,256,512]{2,1,0:T(8,128)(2,1)}, u32[]{:S(2)}, u32[]{:S(2)}) collective-permute-start(bf16[2,256,512]{2,1,0:T(8,128)(2,1)} %get-tuple-element.83), channel_id=1, source_target_pairs={{1,0},{0,1},{3,2},{2,3},{5,4},{4,5},{7,6},{6,7},{9,8},{8,9},{11,10... | collective-permute-start | bytes 1572872 | tf_op jit(solution)/shard_map/ppermute | solution.py:959
  370.9 51.3 %collective-permute-start.37 = (bf16[2,512,512]{2,1,0:T(8,128)(2,1)S(1)}, bf16[2,512,512]{2,1,0:T(8,128)(2,1)}, u32[]{:S(2)}, u32[]{:S(2)}) collective-permute-start(bf16[2,512,512]{2,1,0:T(8,128)(2,1)S(1)} %copy-done.18), channel_id=1, source_target_pairs={{1,0},{0,1},{3,2},{2,3},{5,4},{4,5},{7,6},{6,7},{9,8},{8,9},{11,10... | collective-permute-start | bytes 3145736 | tf_op jit(solution)/shard_map/ppermute | solution.py:959
  419.5 61.2 %collective-permute-start.78 = (bf16[2,3,704,256]{3,2,1,0:T(8,128)(2,1)}, bf16[2,3,704,256]{3,2,1,0:T(8,128)(2,1)}, u32[]{:S(2)}, u32[]{:S(2)}) collective-permute-start(bf16[2,3,704,256]{3,2,1,0:T(8,128)(2,1)} %get-tuple-element.95), channel_id=1, source_target_pairs={{0,8},{8,0},{16,24},{24,16},{1,9},{9,1},{17,25},{25,17},{2,10},{10... | collective-permute-start | bytes 6488072 | tf_op jit(solution)/shard_map/ppermute | solution.py:771
  431.4 37.2 %collective-permute-start.48 = (f32[4,112]{1,0:T(4,128)S(1)}, f32[4,112]{1,0:T(4,128)S(1)}, u32[]{:S(2)}, u32[]{:S(2)}) collective-permute-start(f32[4,112]{1,0:T(4,128)S(1)} %get-tuple-element.175), channel_id=1, source_target_pairs={{0,24},{8,16},{16,8},{24,0},{1,25},{9,17},{17,9},{25,1},{2,26},{10... | collective-permute-start | bytes 5384 | tf_op jit(solution)/shard_map/ppermute | solution.py:804
  432.3 36.2 %collective-permute-start.47 = (f32[4,112]{1,0:T(4,128)S(1)}, f32[4,112]{1,0:T(4,128)S(1)}, u32[]{:S(2)}, u32[]{:S(2)}) collective-permute-start(f32[4,112]{1,0:T(4,128)S(1)} %get-tuple-element.176), channel_id=1, source_target_pairs={{0,16},{8,24},{16,0},{24,8},{1,17},{9,25},{17,1},{25,9},{2,18},{10... | collective-permute-start | bytes 5384 | tf_op jit(solution)/shard_map/ppermute | solution.py:804
  433.4 35.1 %collective-permute-start.46 = (f32[4,112]{1,0:T(4,128)S(1)}, f32[4,112]{1,0:T(4,128)S(1)}, u32[]{:S(2)}, u32[]{:S(2)}) collective-permute-start(f32[4,112]{1,0:T(4,128)S(1)} %get-tuple-element.174), channel_id=1, source_target_pairs={{0,8},{8,0},{16,24},{24,16},{1,9},{9,1},{17,25},{25,17},{2,10},{10... | collective-permute-start | bytes 5384 | tf_op jit(solution)/shard_map/ppermute | solution.py:804
  484.3 46.7 %collective-permute-start.65 = (bf16[4,256,1024]{2,1,0:T(8,128)(2,1)S(1)}, bf16[4,256,1024]{2,1,0:T(8,128)(2,1)S(1)}, u32[]{:S(2)}, u32[]{:S(2)}) collective-permute-start(bf16[4,256,1024]{2,1,0:T(8,128)(2,1)S(1)} %copy-done.97), channel_id=1, source_target_pairs={{0,1},{1,0},{2,3},{3,2},{4,5},{5,4},{6,7},{7,6},{8,9},{9,8},{10,11... | collective-permute-start | bytes 6291464 | tf_op jit(solution)/shard_map/ppermute | solution.py:737
  497.1 40.1 %collective-permute-start.71 = (bf16[4,256,1024]{2,1,0:T(8,128)(2,1)S(1)}, bf16[4,256,1024]{2,1,0:T(8,128)(2,1)S(1)}, u32[]{:S(2)}, u32[]{:S(2)}) collective-permute-start(bf16[4,256,1024]{2,1,0:T(8,128)(2,1)S(1)} %copy-done.96), channel_id=1, source_target_pairs={{0,1},{1,0},{2,3},{3,2},{4,5},{5,4},{6,7},{7,6},{8,9},{9,8},{10,11... | collective-permute-start | bytes 6291464 | tf_op jit(solution)/shard_map/ppermute | solution.py:737
  500.0 30.1 %collective-permute-start.53 = (bf16[2,256,512]{2,1,0:T(8,128)(2,1)S(1)}, bf16[2,256,512]{2,1,0:T(8,128)(2,1)S(1)}, u32[]{:S(2)}, u32[]{:S(2)}) collective-permute-start(bf16[2,256,512]{2,1,0:T(8,128)(2,1)S(1)} %get-tuple-element.113), channel_id=1, source_target_pairs={{0,8},{8,0},{16,24},{24,16},{1,9},{9,1},{17,25},{25,17},{2,10},{10... | collective-permute-start | bytes 1572872 | tf_op jit(solution)/shard_map/ppermute | solution.py:771
  507.5 28.6 %collective-permute-start.59 = (bf16[2,256,512]{2,1,0:T(8,128)(2,1)S(1)}, bf16[2,256,512]{2,1,0:T(8,128)(2,1)S(1)}, u32[]{:S(2)}, u32[]{:S(2)}) collective-permute-start(bf16[2,256,512]{2,1,0:T(8,128)(2,1)S(1)} %get-tuple-element.111), channel_id=1, source_target_pairs={{0,16},{8,24},{16,0},{24,8},{1,17},{9,25},{17,1},{25,9},{2,18},{10... | collective-permute-start | bytes 1572872 | tf_op jit(solution)/shard_map/ppermute | solution.py:771
  530.1 33.8 %collective-permute-start.83 = (bf16[3,352,256]{2,1,0:T(8,128)(2,1)S(1)}, bf16[3,352,256]{2,1,0:T(8,128)(2,1)S(1)}, u32[]{:S(2)}, u32[]{:S(2)}) collective-permute-start(bf16[3,352,256]{2,1,0:T(8,128)(2,1)S(1)} %get-tuple-element.118), channel_id=1, source_target_pairs={{0,4},{1,5},{2,6},{3,7},{4,0},{5,1},{6,2},{7,3},{8,12},{9,13},{10,... | collective-permute-start | bytes 1622024 | tf_op jit(solution)/shard_map/ppermute | solution.py:790
  531.0 33.9 %collective-permute-start.80 = (bf16[3,352,256]{2,1,0:T(8,128)(2,1)S(1)}, bf16[3,352,256]{2,1,0:T(8,128)(2,1)S(1)}, u32[]{:S(2)}, u32[]{:S(2)}) collective-permute-start(bf16[3,352,256]{2,1,0:T(8,128)(2,1)S(1)} %slice_bitcast_fusion.2), channel_id=1, source_target_pairs={{0,6},{1,7},{2,0},{3,1},{4,2},{5,3},{6,4},{7,5},{8,14},{9,15},{10,... | collective-permute-start | bytes 1622024 | tf_op jit(solution)/shard_map/ppermute | solution.py:790
  536.1 29.1 %collective-permute-start.54 = (bf16[1,256,512]{2,1,0:T(8,128)(2,1)S(1)}, bf16[1,256,512]{2,1,0:T(8,128)(2,1)S(1)}, u32[]{:S(2)}, u32[]{:S(2)}) collective-permute-start(bf16[1,256,512]{2,1,0:T(8,128)(2,1)S(1)} %add_convert_fusion.27), channel_id=1, source_target_pairs={{0,16},{8,24},{16,0},{24,8},{1,17},{9,25},{17,1},{25,9},{2,18},{10... | collective-permute-start | bytes 786440 | tf_op jit(solution)/shard_map/ppermute | solution.py:771
  537.3 42.2 %collective-permute-start.60 = (bf16[1,256,512]{2,1,0:T(8,128)(2,1)S(1)}, bf16[1,256,512]{2,1,0:T(8,128)(2,1)S(1)}, u32[]{:S(2)}, u32[]{:S(2)}) collective-permute-start(bf16[1,256,512]{2,1,0:T(8,128)(2,1)S(1)} %add_convert_fusion.24), channel_id=1, source_target_pairs={{0,8},{8,0},{16,24},{24,16},{1,9},{9,1},{17,25},{25,17},{2,10},{10... | collective-permute-start | bytes 786440 | tf_op jit(solution)/shard_map/ppermute | solution.py:771
  542.4 51.4 %collective-permute-start.66 = (bf16[2,256,1024]{2,1,0:T(8,128)(2,1)S(1)}, bf16[2,256,1024]{2,1,0:T(8,128)(2,1)S(1)}, u32[]{:S(2)}, u32[]{:S(2)}) collective-permute-start(bf16[2,256,1024]{2,1,0:T(8,128)(2,1)S(1)} %get-tuple-element.109), channel_id=1, source_target_pairs={{0,8},{8,0},{16,24},{24,16},{1,9},{9,1},{17,25},{25,17},{2,10},{10... | collective-permute-start | bytes 3145736 | tf_op jit(solution)/shard_map/ppermute | solution.py:771
  563.9 31.4 %collective-permute-start.72 = (bf16[2,256,1024]{2,1,0:T(8,128)(2,1)S(1)}, bf16[2,256,1024]{2,1,0:T(8,128)(2,1)S(1)}, u32[]{:S(2)}, u32[]{:S(2)}) collective-permute-start(bf16[2,256,1024]{2,1,0:T(8,128)(2,1)S(1)} %get-tuple-element.107), channel_id=1, source_target_pairs={{0,16},{8,24},{16,0},{24,8},{1,17},{9,25},{17,1},{25,9},{2,18},{10... | collective-permute-start | bytes 3145736 | tf_op jit(solution)/shard_map/ppermute | solution.py:771
  (153 other events, 1761.3 us)
